TPU v7x, 32 devices: a whole 2x2x4 slice. The times are simulated.
32 devices in a mesh: member: 2 (over x), tile: 8 (over z, core), grp: 2 (over y).
Axes of the slice: x: 2, y: 2, z: 4, core: 2. Of those that a mesh axis runs over, the one named last changes fastest.
Arguments:
- latent: bfloat16 [4096, 768], P('tile'), may hold values from -6 to 6
- noise: bfloat16 [4, 4096, 768], P(('member', 'grp'), 'tile'), may hold values from -6 to 6
- area: float32 [4096], P('tile'), may hold values from 0.3 to 9, as said below
- target: float32 [13], replicated, may hold values from -1 to 1
- truth: float32 [80, 4096], P(('member', 'grp'), 'tile'), may hold values from -6 to 6
- neighbours: int32 [4096, 4], P('tile'), may hold values from 0 to 4095, as said below
- w_up: bfloat16 [2, 768, 1536], P(None, 'tile'), may hold values from -0.21875 to 0.21875
- w_down: bfloat16 [2, 1536, 768], P(None, 'tile'), may hold values from -0.15625 to 0.15625
- w_out: bfloat16 [768, 80], P('tile'), may hold values from -0.21875 to 0.21875
Outputs:
- score: float32 [80, 4096], P(('member', 'grp'), 'tile')
- grad_up: float32 [2, 768, 1536], P(None, 'tile')
- grad_down: float32 [2, 1536, 768], P(None, 'tile')
- grad_out: float32 [768, 80], P('tile')
Inputs may be any that keep to these rules, and one draw needn't show every extreme that they name: neighbours[i, k] lies within 32 steps of i in the cyclic order of nodes; for every node one neighbour is exactly 32 steps ahead and another exactly 32 steps behind. `area`: positive.
All inputs are finite; a program needn't handle non-finite values.
Results may differ from a plain program's by a relative error of at most 0.0045.
Values may be sent and summed in bfloat16 or wider, within the bound.
A program may use at most 128 MiB of HBM per device.

v0:
```python
import jax
import jax.numpy as jnp
from jax import lax
from jax.sharding import PartitionSpec as P

TEMP = 13
NEIGH = 4
HALO = 32
LAYERS = 2


EPSILON = 1e-06
SOFTNESS = 0.25
SOFT_ROOT = 0.5


def padded(cells, sides, width):
    for axis, dim in sides:
        count = lax.axis_size(axis)
        head = lax.slice_in_dim(cells, 0, width, axis=dim)
        tail = lax.slice_in_dim(cells, cells.shape[dim] - width, cells.shape[dim], axis=dim)
        cells = jnp.concatenate(
            [
                lax.ppermute(tail, axis, [(i, (i + 1) % count) for i in range(count)]),
                cells,
                lax.ppermute(head, axis, [((i + 1) % count, i) for i in range(count)]),
            ],
            axis=dim,
        )
    return cells


def passed_along(block, axis, distance):
    devices = range(lax.axis_size(axis))
    route = [((i - distance) % len(devices), i) for i in devices]
    return lax.ppermute(block, axis, route)


def normalize(values):
    return values * lax.rsqrt(jnp.mean(values * values, axis=-1, keepdims=True) + EPSILON)


def distance_kernel(offset):
    return jnp.sqrt(offset * offset + SOFTNESS) - SOFT_ROOT


def kernel_slope(offset):
    return offset / jnp.sqrt(offset * offset + SOFTNESS)


def blend_local(normed, local_index):
    extended = padded(normed, (("tile", 0),), HALO)
    summed = extended[local_index[:, 0]].astype(jnp.float32)
    for column in range(1, NEIGH):
        summed = summed + extended[local_index[:, column]].astype(jnp.float32)
    return (normed.astype(jnp.float32) + summed / NEIGH).astype(jnp.bfloat16)


def unblend_local(grad_blend, local_index):
    nodes_dev = grad_blend.shape[0]
    extended = jnp.zeros((nodes_dev + 2 * HALO, grad_blend.shape[1]), jnp.float32)
    portion = grad_blend / NEIGH
    for column in range(NEIGH):
        extended = extended.at[local_index[:, column]].add(portion)
    from_next = passed_along(extended[:HALO], "tile", -1)
    from_prev = passed_along(extended[nodes_dev + HALO :], "tile", 1)
    result = grad_blend + extended[HALO : nodes_dev + HALO]
    result = result.at[nodes_dev - HALO :].add(from_next)
    return result.at[:HALO].add(from_prev)


def shards(latent, noise, area, target, truth, neighbours, w_up, w_down, w_out):
    nodes_dev = latent.shape[0]
    total_nodes = nodes_dev * lax.axis_size("tile")
    row_ids = jnp.arange(nodes_dev, dtype=jnp.int32)
    global_rows = lax.axis_index("tile") * nodes_dev + row_ids
    local_index = (neighbours - global_rows[:, None] + HALO) % total_nodes + row_ids[:, None]
    full_up, full_down, full_out = (
        lax.all_gather(w_up, "tile", axis=1, tiled=True),
        lax.all_gather(w_down, "tile", axis=1, tiled=True),
        lax.all_gather(w_out, "tile", axis=0, tiled=True),
    )
    hidden_state = latent.astype(jnp.float32) + noise[0].astype(jnp.float32)
    stored = []
    for layer_index in range(LAYERS):
        blended = blend_local(normalize(hidden_state).astype(jnp.bfloat16), local_index)
        preact = jnp.dot(blended, full_up[layer_index], preferred_element_type=jnp.float32)
        hidden = jax.nn.gelu(preact).astype(jnp.bfloat16)
        stored.append((hidden_state, blended, preact, hidden))
        hidden_state = hidden_state + jnp.dot(
            hidden, full_down[layer_index], preferred_element_type=jnp.float32
        )
    final_state = hidden_state
    final_normed = normalize(final_state).astype(jnp.bfloat16)
    predicted = jnp.dot(final_normed, full_out, preferred_element_type=jnp.float32)
    channels = predicted.shape[1]
    block_size = channels // lax.axis_size(("member", "grp"))
    first_channel = lax.axis_index(("member", "grp")) * block_size
    is_temp = first_channel + jnp.arange(block_size, dtype=jnp.int32) < TEMP
    weighted, area_total = lax.psum(
        (jnp.dot(area, predicted[:, :TEMP], precision=lax.Precision.HIGHEST), jnp.sum(area)), "tile"
    )
    nudged = predicted.at[:, :TEMP].add(target - weighted / area_total)
    ensemble = lax.all_to_all(
        nudged.T[None], ("member", "grp"), split_axis=1, concat_axis=0, tiled=True
    )
    members = ensemble.shape[0]
    against = ensemble - truth[None]
    skill_term = jnp.mean(distance_kernel(against), axis=0)
    pair_gaps = ensemble[:, None] - ensemble[None, :]
    spread = jnp.sum(distance_kernel(pair_gaps), axis=(0, 1))
    slope_sum = jnp.sum(kernel_slope(pair_gaps), axis=1)
    score_field = skill_term - spread / (2 * members * (members - 1))
    cotangent = kernel_slope(against) / members - slope_sum / (members * (members - 1))
    column_sums = lax.psum(jnp.sum(cotangent, axis=2), "tile")
    correction = jnp.where(is_temp[None, :], column_sums, 0.0)
    cotangent = cotangent - area[None, None, :] * (correction[:, :, None] / area_total)
    returned = lax.all_to_all(
        cotangent, ("member", "grp"), split_axis=0, concat_axis=1, tiled=True
    )[0]
    upstream = returned.T.astype(jnp.bfloat16)
    grad_output = jnp.dot(final_normed.T, upstream, preferred_element_type=jnp.float32)
    grad_final = jnp.dot(upstream, full_out.T, preferred_element_type=jnp.float32)
    grad_state = jax.vjp(normalize, final_state)[1](grad_final)[0]
    ups_list = []
    downs_list = []
    for layer_index in reversed(range(LAYERS)):
        hidden_state, blended, preact, hidden = stored[layer_index]
        flowing = grad_state.astype(jnp.bfloat16)
        downs_list.insert(0, jnp.dot(hidden.T, flowing, preferred_element_type=jnp.float32))
        grad_hidden = jnp.dot(flowing, full_down[layer_index].T, preferred_element_type=jnp.float32)
        grad_preact = jax.vjp(jax.nn.gelu, preact)[1](grad_hidden)[0].astype(jnp.bfloat16)
        ups_list.insert(0, jnp.dot(blended.T, grad_preact, preferred_element_type=jnp.float32))
        grad_blend = jnp.dot(
            grad_preact, full_up[layer_index].T, preferred_element_type=jnp.float32
        )
        grad_normed = unblend_local(grad_blend, local_index)
        grad_state = grad_state + jax.vjp(normalize, hidden_state)[1](grad_normed)[0]
    local_up = jnp.stack(ups_list)
    local_down = jnp.stack(downs_list)
    shard_up, shard_down, shard_out = (
        lax.psum_scatter(local_up, "tile", scatter_dimension=1, tiled=True),
        lax.psum_scatter(local_down, "tile", scatter_dimension=1, tiled=True),
        lax.psum_scatter(grad_output, "tile", scatter_dimension=0, tiled=True),
    )
    sum_up, sum_down, sum_out = lax.psum((shard_up, shard_down, shard_out), ("member", "grp"))
    return (score_field, sum_up, sum_down, sum_out)


def solution(mesh):
    return jax.shard_map(
        shards,
        mesh=mesh,
        in_specs=(
            P("tile", None),
            P(("member", "grp"), "tile", None),
            P("tile"),
            P(),
            P(("member", "grp"), "tile"),
            P("tile", None),
            P(None, "tile", None),
            P(None, "tile", None),
            P("tile", None),
        ),
        out_specs=(
            P(("member", "grp"), "tile"),
            P(None, "tile", None),
            P(None, "tile", None),
            P("tile", None),
        ),
        check_vma=False,
    )
```

profile of v0, /device:TPU:8, one launch (start us, length us, event | category | flops | bytes accessed | tf_op | source)
XLA Modules:
  0.0 579.0 jit_solution(4406345680909058866)
XLA Ops:
  7.2 0.7 all-gather.4.cloned.1.call-update
  8.0 0.7 all-gather.6.cloned.1.call-update
  8.7 1.7 multiply_reduce_fusion.4
  10.8 1.7 collective-permute-start.1
  13.1 1.1 collective-permute-done
  14.3 2.7 gather_fusion.3
  17.0 2.7 gather_fusion.2
  19.8 2.7 gather_fusion.1
  22.5 2.7 gather_fusion
  25.2 2.4 add_convert_fusion.1
  27.6 33.4 %all-gather.4.cloned.1.call-done = bf16[2,768,1536]{2,1,0:T(8,128)(2,1)} async-done(((bf16[2,96,1536]{2,1,0:T(8,128)(2,1)}), bf16[2,768,1536]{2,1,0:T(8,128)(2,1)}) %all-gather.4.cloned.1.call-update) | async-done | bytes 4718608 | tf_op jit(solution)/shard_map/all_gather | solution.py:79
  61.0 4.7 fusion.14
  65.6 47.5 %all-gather.6.cloned.1.call-done = bf16[2,1536,768]{2,1,0:T(8,128)(2,1)} async-done(((bf16[2,192,768]{2,1,0:T(8,128)(2,1)}), bf16[2,1536,768]{2,1,0:T(8,128)(2,1)}) %all-gather.6.cloned.1.call-update) | async-done | bytes 4718608 | tf_op jit(solution)/shard_map/all_gather | solution.py:80
  113.1 4.7 multiply_reduce_fusion.3
  118.3 1.7 collective-permute-start.3
  120.1 14.0 %all-gather = bf16[8,96,80]{1,2,0:T(8,128)(2,1)S(1)} all-gather(bf16[1,96,80]{1,2,0:T(8,128)(2,1)S(1)} %bitcast.72), channel_id=1, replica_groups=mesh['member'=2,'tile'=8,'grp'=2] {'tile'}, dimensions={0}, use_global_device_ids=true | all-gather | bytes 138240 | tf_op jit(solution)/shard_map/all_gather | solution.py:81
  134.3 0.7 reduce_sum.97
  135.0 0.7 compare_reduce_fusion
  135.7 2.0 gather_fusion.7
  137.8 2.7 gather_fusion.6
  140.5 2.7 gather_fusion.5
  143.2 2.7 gather_fusion.4
  145.9 2.1 add_convert_fusion
  148.1 3.4 fusion.18
  151.5 4.9 multiply_reduce_fusion.2
  157.0 14.4 %all-reduce = (f32[13]{0:T(128)S(1)}, f32[]{:T(128)}) all-reduce(f32[13]{0:T(128)S(1)} %convolution_bitcast_fusion.4, f32[]{:T(128)} %reduce_sum.97), channel_id=1, replica_groups=mesh['member'=2,'tile'=8,'grp'=2] {'tile'}, use_global_device_ids=true, to_apply=%region_4.5 | all-reduce | flops 14 | bytes 112 | tf_op jit(solution)/shard_map/psum | solution.py:100
  172.1 0.7 add_select_fusion
  173.1 0.8 copy.18
  173.9 3.7 all-to-all-start
  177.7 5.0 all-to-all-done
  183.2 1.3 fusion.41
  184.8 13.5 %psum.44 = f32[4,20]{1,0:T(4,128)S(1)} all-reduce(f32[4,20]{1,0:T(4,128)S(1)} %reduce_sum.116), channel_id=1, replica_groups=mesh['member'=2,'tile'=8,'grp'=2] {'tile'}, use_global_device_ids=true, to_apply=%region_11.12 | all-reduce | flops 80 | bytes 640 | tf_op jit(solution)/shard_map/psum | solution.py:115
  198.3 0.6 select_divide_fusion
  199.1 7.5 %all_to_all.21 = bf16[4,20,512]{2,1,0:T(8,128)(2,1)S(1)} all-to-all(bf16[4,20,512]{2,1,0:T(8,128)(2,1)S(1)} %multiply_subtract_fusion), channel_id=1, replica_groups=mesh['member'=2,'tile'=8,'grp'=2] {'member','grp'}, dimensions={0} | all-to-all | bytes 163840 | tf_op jit(solution)/shard_map/all_to_all | solution.py:118
  207.4 1.1 copy-done.28
  208.5 3.9 convolution_bitcast_fusion
  212.5 3.0 fusion.13
  215.5 1.2 copy-done.9
  216.7 1.4 fusion.17
  218.1 5.4 scatter_custom_fusion
  223.5 7.1 %scatter_custom_fusion.1 = f32[576,768]{1,0:T(8,128)} fusion(f32[576,768]{1,0:T(8,128)} %scatter_custom_fusion, s32[512]{0:T(512)} %bitcast.79, f32[512,768]{1,0:T(8,128)S(1)} %fusion.17, f32[]{:T(128)} %constant.154.clone.1), kind=kCustom, calls=%fused_computation.71 | custom fusion | flops 786432 | bytes 3342848 | tf_op jit(solution)/shard_map/scatter-add | solution.py:64
  230.6 6.7 %scatter_custom_fusion.2 = f32[576,768]{1,0:T(8,128)} fusion(f32[576,768]{1,0:T(8,128)} %scatter_custom_fusion.1, s32[512]{0:T(512)} %bitcast.77, f32[512,768]{1,0:T(8,128)S(1)} %fusion.17, f32[]{:T(128)} %constant.154.clone.1), kind=kCustom, calls=%fused_computation.69 | custom fusion | flops 786432 | bytes 3342848 | tf_op jit(solution)/shard_map/scatter-add | solution.py:64
  237.3 6.7 %scatter_custom_fusion.3 = f32[576,768]{1,0:T(8,128)} fusion(f32[576,768]{1,0:T(8,128)} %scatter_custom_fusion.2, s32[512]{0:T(512)} %bitcast.75, f32[512,768]{1,0:T(8,128)S(1)} %fusion.17, f32[]{:T(128)} %constant.154.clone.1), kind=kCustom, calls=%fused_computation.67 | custom fusion | flops 786432 | bytes 3342848 | tf_op jit(solution)/shard_map/scatter-add | solution.py:64
  244.1 1.0 fusion.60
  245.0 2.5 collective-permute-start.4
  247.5 1.6 slice_add_fusion
  249.7 3.5 collective-permute-done.5
  253.9 1.3 copy-done.26
  255.1 1.7 convolution_bitcast_fusion.1
  256.9 4.2 pad_maximum_fusion.1
  261.4 0.9 copy-done.6
  262.3 5.0 convolution_bitcast_fusion.2
  267.3 8.9 %convolution_bitcast_fusion.3 = f32[1,768,1536]{2,1,0:T(8,128)} fusion(bf16[512,768]{1,0:T(8,128)(2,1)S(1)} %copy-done.12, f32[512,1536]{1,0:T(8,128)} %fusion.14, bf16[512,768]{1,0:T(8,128)(2,1)} %copy-done.13, bf16[2,1536,768]{2,1,0:T(8,128)(2,1)} %all-gather.6.cloned.1.call-done), kind=kOutput, calls=%fused_computation.21 | convolution fusion | flops 2431647744 | bytes 11796480 | tf_op jit(solution)/shard_map/dot_general | solution.py:133
  276.1 8.4 %pad_maximum_fusion = f32[2,768,1536]{2,1,0:T(8,128)} fusion(f32[1,768,1536]{2,1,0:T(8,128)} %convolution_bitcast_fusion.2, f32[1,768,1536]{2,1,0:T(8,128)} %convolution_bitcast_fusion.3), kind=kLoop, calls=%fused_computation.12 | loop fusion | flops 2359296 | bytes 18874368 | tf_op jit(solution)/shard_map/stack | solution.py:139
  284.6 1.3 fusion.58
  286.0 71.6 %reduce-scatter.8.cloned.1.call-done = f32[2,192,768]{2,1,0:T(8,128)} async-done(((f32[2,1536,768]{2,1,0:T(8,128)}), f32[2,192,768]{2,1,0:T(8,128)}) %reduce-scatter.8.cloned.1.call-update) | async-done | bytes 1179664 | tf_op jit(solution)/shard_map/reduce_scatter | solution.py:143
  357.6 100.1 %reduce-scatter.6.cloned.1.call-done = f32[2,96,1536]{2,1,0:T(8,128)} async-done(((f32[2,768,1536]{2,1,0:T(8,128)}), f32[2,96,1536]{2,1,0:T(8,128)}) %reduce-scatter.6.cloned.1.call-update) | async-done | bytes 1179664 | tf_op jit(solution)/shard_map/reduce_scatter | solution.py:142
  457.7 0.6 multiply_subtract_fusion.1
  458.4 30.3 %reduce-scatter.10.cloned.1.call-done = f32[96,80]{1,0:T(8,128)} async-done(((f32[768,80]{1,0:T(8,128)}), f32[96,80]{1,0:T(8,128)}) %reduce-scatter.10.cloned.1.call-update) | async-done | bytes 30736
  488.6 0.9 copy.22
  489.5 17.2 %psum.47 = f32[96,80]{0,1:T(8,128)} all-reduce(f32[96,80]{0,1:T(8,128)S(1)} %copy.22), channel_id=1, replica_groups=mesh['member'=2,'tile'=8,'grp'=2] {'member','grp'}, use_global_device_ids=true, to_apply=%region_23.24 | all-reduce | flops 7680 | bytes 61440 | tf_op jit(solution)/shard_map/psum | solution.py:146
  506.8 61.7 %all-reduce.4.cloned.1.call-done = (f32[2,96,1536]{2,1,0:T(8,128)}, f32[2,192,768]{2,1,0:T(8,128)}) async-done(((f32[2,96,1536]{2,1,0:T(8,128)}, f32[2,192,768]{2,1,0:T(8,128)}), (f32[2,96,1536]{2,1,0:T(8,128)}, f32[2,192,768]{2,1,0:T(8,128)})) %all-reduce.4.cloned.1.call-update) | async-done | bytes 2359312 | tf_op jit(solution)/shard_map/psum | solution.py:146
  568.5 2.5 copy.35
  571.0 1.0 copy.36
  (129 shorter events, 6.9 us)
Async XLA Ops:
  7.2 3.2 copy-start.8
  7.2 3.2 copy-start.7
  7.2 53.8 %all-gather.4.cloned.1.call-start = ((), (), s32[]{:S(2)}) async-start(), calls=%async_computation.5 | async-start | bytes 5308416 | tf_op jit(solution)/shard_map/all_gather | solution.py:79
  7.9 105.2 %all-gather.6.cloned.1.call-start = ((), (), s32[]{:S(2)}) async-start(), calls=%async_computation.6 | async-start | bytes 5308416 | tf_op jit(solution)/shard_map/all_gather | solution.py:80
  8.7 3.8 copy-start.20
  10.7 3.6 collective-permute-start
  10.8 3.5 collective-permute-start.1
  12.5 0.6 copy-start.24
  12.5 4.5 copy-start.21
  12.6 4.5 copy-start.22
  12.6 4.5 copy-start.23
  27.6 38.1 %copy-start.11 = (bf16[512,768]{1,0:T(8,128)(2,1)}, bf16[512,768]{1,0:T(8,128)(2,1)S(1)}, u32[]{:S(2)}) copy-start(bf16[512,768]{1,0:T(8,128)(2,1)S(1)} %add_convert_fusion.1) | copy-start | bytes 2359300
  117.8 17.9 %copy-start.18 = (f32[512]{0:T(512)}, f32[512]{0:T(512)S(1)}, u32[]{:S(2)}) copy-start(f32[512]{0:T(512)S(1)} %get-tuple-element.56) | copy-start | bytes 6148
  117.8 28.1 %copy-start = (f32[512,768]{1,0:T(8,128)}, f32[512,768]{1,0:T(8,128)S(1)}, u32[]{:S(2)}) copy-start(f32[512,768]{1,0:T(8,128)S(1)} %get-tuple-element.57) | copy-start | bytes 4718596
  117.8 2.2 copy-start.15
  117.8 16.5 %copy-start.16 = (f32[512]{0:T(512)S(1)}, f32[512]{0:T(512)}, u32[]{:S(2)}) copy-start(f32[512]{0:T(512)} %param.17) | copy-start | bytes 6148
  118.0 17.6 %collective-permute-start.2 = (bf16[32,768]{1,0:T(8,128)(2,1)S(1)}, bf16[32,768]{1,0:T(8,128)(2,1)S(1)}, u32[]{:S(2)}, u32[]{:S(2)}) collective-permute-start(bf16[32,768]{1,0:T(8,128)(2,1)S(1)} %get-tuple-element.48), channel_id=1, source_target_pairs={{0,2},{2,4},{4,6},{6,8},{8,10},{10,12},{12,14},{14,0},{1,3},{3,5},... | collective-permute-start | bytes 147464 | tf_op jit(solution)/shard_map/ppermute | solution.py:24
  118.3 17.3 %collective-permute-start.3 = (bf16[32,768]{1,0:T(8,128)(2,1)S(1)}, bf16[32,768]{1,0:T(8,128)(2,1)S(1)}, u32[]{:S(2)}, u32[]{:S(2)}) collective-permute-start(bf16[32,768]{1,0:T(8,128)(2,1)S(1)} %get-tuple-element.49), channel_id=1, source_target_pairs={{2,0},{4,2},{6,4},{8,6},{10,8},{12,10},{14,12},{0,14},{3,1},{5,3},... | collective-permute-start | bytes 147464 | tf_op jit(solution)/shard_map/ppermute | solution.py:26
  148.0 3.4 copy-start.5
  148.1 3.4 copy-start.1
  151.5 4.9 copy-start.27
  156.3 15.1 %copy-start.25 = (f32[13]{0:T(128)S(1)}, f32[13]{0:T(128)}, u32[]{:S(2)}) copy-start(f32[13]{0:T(128)} %param.18) | copy-start | bytes 160
  156.4 21.2 %copy-start.14 = (f32[20,512]{1,0:T(8,128)S(1)}, f32[20,512]{1,0:T(8,128)}, u32[]{:S(2)}) copy-start(f32[20,512]{1,0:T(8,128)} %param.19) | copy-start | bytes 122884
  173.9 8.8 %all-to-all-start = ((f32[1,80,512]{2,0,1:T(1,128)}), f32[1,80,512]{2,0,1:T(1,128)S(1)}, u32[]{:S(2)}, u32[]{:S(2)}) async-start(f32[1,80,512]{2,0,1:T(1,128)} %copy.18), calls=%async_computation | async-start | bytes 327680 | tf_op jit(solution)/shard_map/all_to_all | solution.py:104
  177.6 21.3 %copy-start.17 = (f32[512]{0:T(512)S(1)}, f32[512]{0:T(512)}, u32[]{:S(2)}) copy-start(f32[512]{0:T(512)} %param.17) | copy-start | bytes 6148
  177.6 180.0 %reduce-scatter.8.cloned.1.call-start = ((), (), s32[]{:S(2)}) async-start(), calls=%async_computation.8 | async-start | bytes 10616832 | tf_op jit(solution)/shard_map/reduce_scatter | solution.py:143
  206.6 1.9 copy-start.28
  207.1 5.3 slice-start.2
  208.5 4.0 copy-start.3
  208.5 4.0 slice-start.3
  208.5 8.2 %slice-start.4 = ((s8[4718592]{0:T(1024)(128)(4,1)}), s8[4194304]{0:T(1024)(128)(4,1)S(1)}, s32[]{:S(2)}) async-start(s8[4718592]{0:T(1024)(128)(4,1)} %bitcast.84), calls=%async_computation.15 | async-start | bytes 8388608
  212.5 4.2 slice-start.5
  215.5 1.2 copy-start.9
  245.0 8.2 %copy-start.2 = (f32[512,768]{1,0:T(8,128)S(1)}, f32[512,768]{1,0:T(8,128)}, u32[]{:S(2)}) copy-start(f32[512,768]{1,0:T(8,128)} %copy-done) | copy-start | bytes 4718596
  245.0 4.7 collective-permute-start.4
  249.1 4.1 collective-permute-start.5
  249.7 3.7 copy-start.19
  249.7 3.8 copy-start.4
  253.2 1.9 copy-start.26
  253.5 3.4 slice-start
  255.1 1.7 copy-start.13
  255.1 1.8 slice-start.1
  261.1 1.1 copy-start.6
  261.2 6.1 %copy-start.12 = (bf16[512,768]{1,0:T(8,128)(2,1)S(1)}, bf16[512,768]{1,0:T(8,128)(2,1)}, u32[]{:S(2)}) copy-start(bf16[512,768]{1,0:T(8,128)(2,1)} %copy-done.11) | copy-start | bytes 2359300
  261.2 196.4 %reduce-scatter.6.cloned.1.call-start = ((), (), s32[]{:S(2)}) async-start(), calls=%async_computation.7 | async-start | bytes 10616832 | tf_op jit(solution)/shard_map/reduce_scatter | solution.py:142
  284.5 204.1 %reduce-scatter.10.cloned.1.call-start = ((), (), s32[]{:S(2)}) async-start(), calls=%async_computation.9 | async-start | bytes 442368
  285.9 282.6 %all-reduce.4.cloned.1.call-start = ((), (), s32[]{:S(2)}) async-start(), calls=%async_computation.10 | async-start | bytes 4718592 | tf_op jit(solution)/shard_map/psum | solution.py:146
  568.5 2.5 copy-start.10
Sparse Core Ops, SparseCore 0:
  9.6 51.2 all-gather.3
  62.6 50.5 all-gather.5
  261.3 96.2 reduce-scatter.7
  359.7 97.8 reduce-scatter.5
  460.3 28.2 reduce-scatter.9
  491.9 76.4 all-reduce.3
where the time goes:
time: 587 us; the launch traced here: 579 us
  waiting for transfers between devices  356 us (61%)
  blocking collectives  66.7 us (11%)
  other arithmetic  53.9 us (9%)
  matrix products  43.9 us (7%)
  local copies, waits for them, and re-layouts  33 us (6%)
  between operations  15 us (3%)
  starting transfers between devices  10.4 us (2%)
    reduce_scatter x1, waiting for transfers between devices, shards(): lax.psum_scatter(local_up, 'tile', scatter_dimension=1, tiled=True)  100 us
    reduce_scatter x1, waiting for transfers between devices, shards(): lax.psum_scatter(local_down, 'tile', scatter_dimension=1, tiled=True)  71.6 us
    psum x1, waiting for transfers between devices, shards(): lax.psum((shard_up, shard_down, shard_out), ('member', 'grp'))  61.7 us
    all_gather x1, waiting for transfers between devices, shards(): lax.all_gather(w_down, 'tile', axis=1, tiled=True)  47.5 us
    all_gather x1, waiting for transfers between devices, shards(): lax.all_gather(w_up, 'tile', axis=1, tiled=True)  33.4 us
    unnamed x7, waiting for transfers between devices  31.7 us
    scatter-add x4, other arithmetic, unblend_local(): extended = extended.at[local_index[:, column]].add(portion)  25.9 us
    psum x1, blocking collectives, shards(): lax.psum((shard_up, shard_down, shard_out), ('member', 'grp'))  17.2 us
  transfers between devices with their start and end apart: 13, of which 10 were waited for; matrix products, arithmetic and copies ran while one was open for 8% of the time, Pallas kernels for 0%

commit v1 on v0

v1 whole, which is shorter than its diff:
```python
import jax
import jax.numpy as jnp
from jax import lax
from jax.sharding import PartitionSpec as P

TEMP = 13
NEIGH = 4
HALO = 32
LAYERS = 2


EPSILON = 1e-06
SOFTNESS = 0.25
SOFT_ROOT = 0.5
SHARE = jnp.bfloat16


def padded(cells, sides, width):
    for axis, dim in sides:
        count = lax.axis_size(axis)
        head = lax.slice_in_dim(cells, 0, width, axis=dim)
        tail = lax.slice_in_dim(cells, cells.shape[dim] - width, cells.shape[dim], axis=dim)
        cells = jnp.concatenate(
            [
                lax.ppermute(tail, axis, [(i, (i + 1) % count) for i in range(count)]),
                cells,
                lax.ppermute(head, axis, [((i + 1) % count, i) for i in range(count)]),
            ],
            axis=dim,
        )
    return cells


def passed_along(block, axis, distance):
    devices = range(lax.axis_size(axis))
    route = [((i - distance) % len(devices), i) for i in devices]
    return lax.ppermute(block, axis, route)


def normalize(values):
    return values * lax.rsqrt(jnp.mean(values * values, axis=-1, keepdims=True) + EPSILON)


def distance_kernel(offset):
    return jnp.sqrt(offset * offset + SOFTNESS) - SOFT_ROOT


def kernel_slope(offset):
    return offset / jnp.sqrt(offset * offset + SOFTNESS)


def paired():
    return lax.axis_size("member") == 2 and lax.axis_size("grp") == 2


def swapped(block, axis):
    return lax.ppermute(block, axis, [(0, 1), (1, 0)])


def core_swapped(block):
    return lax.ppermute(block, "tile", [(i, i ^ 1) for i in range(lax.axis_size("tile"))])


def shifted(block, distance):
    count = lax.axis_size("tile")
    chips = count // 2
    route = [(i, (i // 2 + distance) % chips * 2 + i % 2) for i in range(count)]
    return lax.ppermute(block, "tile", route)


def tile_sum(values):
    count = lax.axis_size("tile")
    if count & (count - 1):
        return lax.psum(values, "tile")
    step = 1
    while step < count:
        values = values + lax.ppermute(values, "tile", [(i, i ^ step) for i in range(count)])
        step *= 2
    return values


def pick(block, index, dim):
    return lax.dynamic_index_in_dim(block, index, dim, keepdims=False)


def half(block, index, dim):
    size = block.shape[dim] // 2
    return lax.dynamic_slice_in_dim(block, index * size, size, axis=dim)


def halved(block, index, dim, axis):
    got = swapped(half(block, 1 - index, dim).astype(jnp.bfloat16), axis)
    return half(block, index, dim) + got.astype(jnp.float32)


def blend_matrix(local_index, nodes_dev):
    column = jnp.arange(nodes_dev + 2 * HALO, dtype=jnp.int32)[None, :]
    row = jnp.arange(nodes_dev, dtype=jnp.int32)[:, None]
    total = (column == row + HALO).astype(jnp.float32)
    for k in range(NEIGH):
        total = total + jnp.where(column == local_index[:, k : k + 1], 1.0 / NEIGH, 0.0)
    return total.astype(jnp.bfloat16)


def blend_local(normed, matrix):
    extended = padded(normed, (("tile", 0),), HALO)
    return jnp.dot(matrix, extended, preferred_element_type=jnp.float32).astype(jnp.bfloat16)


def unblend_local(grad_blend, matrix):
    nodes_dev = grad_blend.shape[0]
    coarse = lax.reduce_precision(grad_blend, 8, 7)
    fine = (grad_blend - coarse).astype(jnp.bfloat16)
    extended = jnp.dot(
        matrix.T, coarse.astype(jnp.bfloat16), preferred_element_type=jnp.float32
    ) + jnp.dot(matrix.T, fine, preferred_element_type=jnp.float32)
    from_next = passed_along(extended[:HALO], "tile", -1)
    from_prev = passed_along(extended[nodes_dev + HALO :], "tile", 1)
    result = extended[HALO : nodes_dev + HALO]
    result = result.at[nodes_dev - HALO :].add(from_next)
    return result.at[:HALO].add(from_prev)


def core_reduced(left, right):
    count = lax.axis_size("tile")
    core = lax.axis_index("tile") % 2
    grouped = left.reshape(left.shape[0], count // 2, 2, -1)
    rows = left.shape[1] // 2

    def product(which):
        chosen = pick(grouped, which, 2).reshape(left.shape[0], rows)
        return jnp.dot(chosen.T, right, preferred_element_type=jnp.float32)

    got = core_swapped(product(1 - core).astype(jnp.bfloat16))
    total = product(core) + got.astype(jnp.float32)
    return total.reshape(count // 2, -1, right.shape[1])


def reduced_widely(down, up):
    chips = lax.axis_size("tile") // 2
    chip = lax.axis_index("tile") // 2
    totals = []
    for parts in (down, up):
        total = pick(parts, chip, 0)
        for k in range(1, chips):
            sent = pick(parts, (chip + k) % chips, 0).astype(jnp.bfloat16)
            total = total + shifted(sent, k).astype(jnp.float32)
        totals.append(lax.psum(total, ("member", "grp")))
    return tuple(totals)


def reduced(down, up):
    if not paired():
        return reduced_widely(down, up)
    chips = lax.axis_size("tile") // 2
    chip = lax.axis_index("tile") // 2
    x = lax.axis_index("member")
    y = lax.axis_index("grp")
    rows = down.shape[1] // 2
    width = down.shape[2]
    first = jnp.stack([down[:, :rows], up[:, :, :width]])
    second = jnp.stack([down[:, rows:], up[:, :, width:]])
    first = halved(first, x, 2, "member")
    second = halved(second, y, 2, "grp")
    first = halved(first, y, 3, "grp")
    second = halved(second, x, 3, "member")
    both = jnp.stack([first, second])
    total = pick(both, chip, 2)
    for k in range(1, chips):
        sent = pick(both, (chip + k) % chips, 2).astype(jnp.bfloat16)
        total = total + shifted(sent, k).astype(jnp.float32)
    own = total.astype(SHARE)
    grid = [(m, g) for m in range(2) for g in range(2)]

    def from_corner(dm, dg):
        if not (dm or dg):
            return own
        route = [(2 * m + g, 2 * (m ^ dm) + (g ^ dg)) for m, g in grid]
        return lax.ppermute(own, ("member", "grp"), route)

    corners = [from_corner(m, g) for m, g in grid]
    west = [jnp.where(x == 0, corners[g], corners[2 + g]) for g in range(2)]
    east = [jnp.where(x == 0, corners[2 + g], corners[g]) for g in range(2)]

    def ordered(pair):
        return (jnp.where(y == 0, pair[0], pair[1]), jnp.where(y == 0, pair[1], pair[0]))

    (a00, a01), (a10, a11) = ordered(west), ordered(east)

    def tiled(p, q, r, s, part):
        top = jnp.concatenate([p[part], q[part]], axis=2)
        low = jnp.concatenate([r[part], s[part]], axis=2)
        return jnp.concatenate([top, low], axis=1).astype(jnp.float32)

    first = tiled(a00, a01, a10, a11, 0)
    second = tiled(a00, a10, a01, a11, 1)
    return (
        jnp.concatenate([first[0], second[0]], axis=0),
        jnp.concatenate([first[1], second[1]], axis=1),
    )


def reduced_out(left, right):
    chips = lax.axis_size("tile") // 2
    chip = lax.axis_index("tile") // 2
    core = lax.axis_index("tile") % 2
    whole = jnp.dot(left.T, right, preferred_element_type=jnp.float32)
    whole = whole.reshape(chips, 2, -1, right.shape[1])
    total = pick(whole, core, 1) + core_swapped(pick(whole, 1 - core, 1))
    mine = pick(total, chip, 0)
    for k in range(1, chips):
        mine = mine + shifted(pick(total, (chip + k) % chips, 0), k)
    if not paired():
        return lax.psum(mine, ("member", "grp"))
    mine = mine + swapped(mine, "member")
    return mine + swapped(mine, "grp")


def gathered_out(block):
    chips = lax.axis_size("tile") // 2
    chip = lax.axis_index("tile") // 2
    core = lax.axis_index("tile") % 2
    other = core_swapped(block)
    pair = jnp.concatenate(
        [jnp.where(core == 0, block, other), jnp.where(core == 0, other, block)], axis=0
    )
    parts = jnp.stack([pair] + [shifted(pair, k) for k in range(1, chips)])
    order = (chip - jnp.arange(chips)) % chips
    return jnp.concatenate([pick(parts, order[z], 0) for z in range(chips)], axis=0)


def shards(latent, noise, area, target, truth, neighbours, w_up, w_down, w_out):
    nodes_dev = latent.shape[0]
    total_nodes = nodes_dev * lax.axis_size("tile")
    row_ids = jnp.arange(nodes_dev, dtype=jnp.int32)
    global_rows = lax.axis_index("tile") * nodes_dev + row_ids
    local_index = (neighbours - global_rows[:, None] + HALO) % total_nodes + row_ids[:, None]
    full_up = [lax.all_gather(w_up[l], "tile", axis=0, tiled=True) for l in range(LAYERS)]
    full_down = [lax.all_gather(w_down[l], "tile", axis=0, tiled=True) for l in range(LAYERS)]
    full_out = gathered_out(w_out)
    matrix = blend_matrix(local_index, nodes_dev)
    hidden_state = latent.astype(jnp.float32) + noise[0].astype(jnp.float32)
    stored = []
    for layer_index in range(LAYERS):
        blended = blend_local(normalize(hidden_state).astype(jnp.bfloat16), matrix)
        preact = jnp.dot(blended, full_up[layer_index], preferred_element_type=jnp.float32)
        hidden = jax.nn.gelu(preact).astype(jnp.bfloat16)
        stored.append((hidden_state, blended, preact, hidden))
        hidden_state = hidden_state + jnp.dot(
            hidden, full_down[layer_index], preferred_element_type=jnp.float32
        )
    final_state = hidden_state
    final_normed = normalize(final_state).astype(jnp.bfloat16)
    predicted = jnp.dot(final_normed, full_out, preferred_element_type=jnp.float32)
    channels = predicted.shape[1]
    block_size = channels // lax.axis_size(("member", "grp"))
    first_channel = lax.axis_index(("member", "grp")) * block_size
    is_temp = first_channel + jnp.arange(block_size, dtype=jnp.int32) < TEMP
    local_sums = jnp.concatenate(
        [
            jnp.dot(area, predicted[:, :TEMP], precision=lax.Precision.HIGHEST),
            jnp.sum(area)[None],
        ]
    )
    sums = tile_sum(local_sums)
    weighted, area_total = sums[:TEMP], sums[TEMP]
    nudged = predicted.at[:, :TEMP].add(target - weighted / area_total)
    ensemble = lax.all_to_all(
        nudged.T[None], ("member", "grp"), split_axis=1, concat_axis=0, tiled=True
    )
    members = ensemble.shape[0]
    against = ensemble - truth[None]
    skill_term = jnp.mean(distance_kernel(against), axis=0)
    pair_gaps = ensemble[:, None] - ensemble[None, :]
    spread = jnp.sum(distance_kernel(pair_gaps), axis=(0, 1))
    slope_sum = jnp.sum(kernel_slope(pair_gaps), axis=1)
    score_field = skill_term - spread / (2 * members * (members - 1))
    cotangent = kernel_slope(against) / members - slope_sum / (members * (members - 1))
    column_sums = tile_sum(jnp.sum(cotangent, axis=2))
    correction = jnp.where(is_temp[None, :], column_sums, 0.0)
    cotangent = cotangent - area[None, None, :] * (correction[:, :, None] / area_total)
    returned = lax.all_to_all(
        cotangent, ("member", "grp"), split_axis=0, concat_axis=1, tiled=True
    )[0]
    upstream = returned.T.astype(jnp.bfloat16)
    sum_out = reduced_out(final_normed, upstream)
    grad_final = jnp.dot(upstream, full_out.T, preferred_element_type=jnp.float32)
    grad_state = jax.vjp(normalize, final_state)[1](grad_final)[0]
    ups_list = []
    downs_list = []
    for layer_index in reversed(range(LAYERS)):
        hidden_state, blended, preact, hidden = stored[layer_index]
        flowing = grad_state.astype(jnp.bfloat16)
        down = core_reduced(hidden, flowing)
        grad_hidden = jnp.dot(flowing, full_down[layer_index].T, preferred_element_type=jnp.float32)
        grad_preact = jax.vjp(jax.nn.gelu, preact)[1](grad_hidden)[0].astype(jnp.bfloat16)
        sum_down, sum_up = reduced(down, core_reduced(blended, grad_preact))
        downs_list.insert(0, sum_down)
        ups_list.insert(0, sum_up)
        if layer_index == 0:
            break
        grad_blend = jnp.dot(
            grad_preact, full_up[layer_index].T, preferred_element_type=jnp.float32
        )
        grad_normed = unblend_local(grad_blend, matrix)
        grad_state = grad_state + jax.vjp(normalize, hidden_state)[1](grad_normed)[0]
    return (score_field, jnp.stack(ups_list), jnp.stack(downs_list), sum_out)


def solution(mesh):
    return jax.shard_map(
        shards,
        mesh=mesh,
        in_specs=(
            P("tile", None),
            P(("member", "grp"), "tile", None),
            P("tile"),
            P(),
            P(("member", "grp"), "tile"),
            P("tile", None),
            P(None, "tile", None),
            P(None, "tile", None),
            P("tile", None),
        ),
        out_specs=(
            P(("member", "grp"), "tile"),
            P(None, "tile", None),
            P(None, "tile", None),
            P("tile", None),
        ),
        check_vma=False,
    )
```

time: 587 us -> 324 us (0.55); the launches traced: 579 us -> 323 us
  waiting for transfers between devices: 356 us -> 154 us
  blocking collectives: 66.7 us -> 0 us
  starting transfers between devices: 10.4 us -> 56 us
  other arithmetic: 53.9 us -> 19.4 us
  between operations: 15 us -> 22.6 us
    reduce_scatter x2 -> x0, waiting for transfers between devices: 172 us -> none  [the longest x1 100 us: shards(): lax.psum_scatter(local_up, 'tile', scatter_dimension=1, tiled=True)]
    psum x1 -> x0, waiting for transfers between devices: 61.7 us -> none  [shards(): lax.psum((shard_up, shard_down, shard_out), ('member', 'grp'))]
    ppermute x0 -> x40, waiting for transfers between devices: none -> 55.8 us  [the longest x10 29 us: swapped(): return lax.ppermute(block, axis, [(0, 1), (1, 0)])]
    psum x3 -> x0, blocking collectives: 45.2 us -> none  [the longest x1 17.2 us: shards(): lax.psum((shard_up, shard_down, shard_out), ('member', 'grp'))]
    ppermute x0 -> x40, starting transfers between devices: none -> 43.3 us  [the longest x12 17.7 us: shifted(): return lax.ppermute(block, 'tile', route)]
    unnamed x7 -> x4, waiting for transfers between devices: 31.7 us -> 0.73 us
    scatter-add x4 -> x0, other arithmetic: 25.9 us -> none  [unblend_local(): extended = extended.at[local_index[:, column]].add(portion)]
    gather x8 -> x0, local copies, waits for them, and re-layouts: 21 us -> none  [the longest x6 15.6 us: blend_local(): summed = summed + extended[local_index[:, column]].astype(jnp.float32)]
  transfers between devices with their start and end apart: 13 -> 52, of which waited for: 10 -> 25; matrix products, arithmetic and copies ran while one was open for 8% -> 15% of each run, Pallas kernels for 0% -> 0%
where the time goes in v1:
time: 324 us; the launch traced here: 323 us
  waiting for transfers between devices  154 us (48%)
  starting transfers between devices  56 us (17%)
  matrix products  41 us (13%)
  local copies, waits for them, and re-layouts  29.5 us (9%)
  between operations  22.6 us (7%)
  other arithmetic  19.4 us (6%)
    all_gather x2, waiting for transfers between devices, shards(): lax.all_gather(w_down[l], 'tile', axis=0, tiled=True)  55.3 us
    all_gather x2, waiting for transfers between devices, shards(): lax.all_gather(w_up[l], 'tile', axis=0, tiled=True)  37.2 us
    ppermute x10, waiting for transfers between devices, swapped(): return lax.ppermute(block, axis, [(0, 1), (1, 0)])  29 us
    ppermute x12, starting transfers between devices, shifted(): return lax.ppermute(block, 'tile', route)  17.7 us
    ppermute x12, waiting for transfers between devices, shifted(): return lax.ppermute(block, 'tile', route)  11.9 us
    dot_general x2, matrix products, shards(): jnp.dot(blended, full_up[layer_index], preferred_element_type=jnp.float32)  11.1 us
    ppermute x6, waiting for transfers between devices, tile_sum(): lax.ppermute(values, 'tile', [(i, i ^ step) for i in range(count)])  10.8 us
    ppermute x10, starting transfers between devices, swapped(): return lax.ppermute(block, axis, [(0, 1), (1, 0)])  10.1 us
  transfers between devices with their start and end apart: 52, of which 25 were waited for; matrix products, arithmetic and copies ran while one was open for 15% of the time, Pallas kernels for 0%

profile of v1, /device:TPU:8, one launch (start us, length us, event | category | flops | bytes accessed | tf_op | source)
XLA Modules:
  0.0 322.8 jit_solution(14614422604089666960)
XLA Ops:
  7.3 2.0 fusion.141
  12.3 1.3 collective-permute-start.1
  14.4 1.6 collective-permute-start.5
  16.1 3.2 %collective-permute-start.6 = (bf16[192,80]{0,1:T(8,128)(2,1)S(1)}, bf16[192,80]{0,1:T(8,128)(2,1)S(1)}, u32[]{:S(2)}, u32[]{:S(2)}) collective-permute-start(bf16[192,80]{0,1:T(8,128)(2,1)S(1)} %get-tuple-element.116), channel_id=1, source_target_pairs={{0,8},{2,10},{4,12},{6,14},{8,0},{10,2},{12,4},{14,6},{1,9},{3,11}... | collective-permute-start | bytes 92168 | tf_op jit(solution)/shard_map/ppermute | solution.py:68
  27.6 1.4 convolution_convert_fusion.5
  29.0 13.1 %all-gather.9.cloned.1.call-done = bf16[1,768,1536]{2,1,0:T(8,128)(2,1)} async-done(((bf16[1,96,1536]{2,1,0:T(8,128)(2,1)}), bf16[1,768,1536]{2,1,0:T(8,128)(2,1)}) %all-gather.9.cloned.1.call-update) | async-done | bytes 2359312 | tf_op jit(solution)/shard_map/all_gather | solution.py:238
  42.0 5.5 %multiply_convert_fusion.1 = (bf16[512,1536]{1,0:T(8,128)(2,1)}, f32[512,1536]{1,0:T(8,128)}) fusion(bf16[512,768]{1,0:T(8,128)(2,1)S(1)} %convolution_convert_fusion.5, bf16[1,768,1536]{2,1,0:T(8,128)(2,1)} %all-gather.9.cloned.1.call-done), kind=kOutput, calls=%fused_computation.19 | convolution fusion | flops 1215037440 | bytes 7864320 | tf_op jit(solution)/shard_map/dot_general | solution.py:246
  47.6 28.5 %all-gather.11.cloned.1.call-done = bf16[1,1536,768]{2,1,0:T(8,128)(2,1)} async-done(((bf16[1,192,768]{2,1,0:T(8,128)(2,1)}), bf16[1,1536,768]{2,1,0:T(8,128)(2,1)}) %all-gather.11.cloned.1.call-update) | async-done | bytes 2359312 | tf_op jit(solution)/shard_map/all_gather | solution.py:239
  76.1 3.6 %multiply_reduce_fusion.3 = (f32[512]{0:T(512)S(1)}, f32[512,768]{1,0:T(8,128)S(1)}) fusion(bf16[512,1536]{1,0:T(8,128)(2,1)} %get-tuple-element.127, bf16[1,1536,768]{2,1,0:T(8,128)(2,1)} %all-gather.11.cloned.1.call-done, bf16[1,512,768]{2,1,0:T(8,128)(2,1)S(1)} %copy-done.5, bf16[512,768]{1,0:T(8,128)(2,1)S(1)} %copy-done.4), kind=kOutput, calls=%fused_computation.85 | convolution fusion | flops 1210318336 | bytes 7079936 | tf_op jit(solution)/shard_map/dot_general | solution.py:249
  80.3 1.4 collective-permute-start.3
  81.8 1.7 collective-permute-done.2
  83.6 1.4 convolution_convert_fusion.4
  85.0 24.1 %all-gather.13.cloned.1.call-done = bf16[1,768,1536]{2,1,0:T(8,128)(2,1)} async-done(((bf16[1,96,1536]{2,1,0:T(8,128)(2,1)}), bf16[1,768,1536]{2,1,0:T(8,128)(2,1)}) %all-gather.13.cloned.1.call-update) | async-done | bytes 2359312 | tf_op jit(solution)/shard_map/all_gather | solution.py:238
  109.1 5.5 %multiply_convert_fusion = (bf16[512,1536]{1,0:T(8,128)(2,1)}, f32[512,1536]{1,0:T(8,128)}) fusion(bf16[512,768]{1,0:T(8,128)(2,1)S(1)} %convolution_convert_fusion.4, bf16[1,768,1536]{2,1,0:T(8,128)(2,1)} %all-gather.13.cloned.1.call-done), kind=kOutput, calls=%fused_computation.18 | convolution fusion | flops 1215037440 | bytes 7864320 | tf_op jit(solution)/shard_map/dot_general | solution.py:246
  114.6 26.7 %all-gather.15.cloned.1.call-done = bf16[1,1536,768]{2,1,0:T(8,128)(2,1)} async-done(((bf16[1,192,768]{2,1,0:T(8,128)(2,1)}), bf16[1,1536,768]{2,1,0:T(8,128)(2,1)}) %all-gather.15.cloned.1.call-update) | async-done | bytes 2359312 | tf_op jit(solution)/shard_map/all_gather | solution.py:239
  141.4 3.6 %multiply_reduce_fusion.2 = (f32[512]{0:T(512)S(1)}, f32[512,768]{1,0:T(8,128)S(1)}) fusion(f32[512,768]{1,0:T(8,128)S(1)} %get-tuple-element.130, bf16[512,1536]{1,0:T(8,128)(2,1)} %get-tuple-element.131, bf16[1,1536,768]{2,1,0:T(8,128)(2,1)} %all-gather.15.cloned.1.call-done), kind=kOutput, calls=%fused_computation.83 | convolution fusion | flops 1209138688 | bytes 7079936 | tf_op jit(solution)/shard_map/dot_general | solution.py:249
  149.3 2.5 collective-permute-done.9
  153.5 2.7 collective-permute-done.10
  159.3 3.6 %all-to-all-start = ((f32[1,80,512]{2,0,1:T(1,128)}), f32[1,80,512]{2,0,1:T(1,128)S(1)}, u32[]{:S(2)}, u32[]{:S(2)}) async-start(f32[1,80,512]{2,0,1:T(1,128)} %copy.39), calls=%async_computation | async-start | bytes 327680 | tf_op jit(solution)/shard_map/all_to_all | solution.py:268
  165.4 1.7 copy.41
  167.1 2.6 copy.46
  171.0 1.9 fusion.72
  173.5 1.6 div.107
  175.1 1.7 subtract_reduce_fusion
  177.6 3.1 constant_dynamic-slice_fusion.5
  180.7 1.5 copy.47
  183.9 1.2 constant_dynamic-slice_fusion.2
  185.1 1.4 collective-permute-done.12
  187.8 3.3 %collective-permute-done.13 = f32[4,20]{1,0:T(4,128)S(1)} collective-permute-done((f32[4,20]{1,0:T(4,128)S(1)}, f32[4,20]{1,0:T(4,128)S(1)}, u32[]{:S(2)}, u32[]{:S(2)}) %collective-permute-start.13) | collective-permute-done | bytes 352 | tf_op jit(solution)/shard_map/ppermute | solution.py:77
  192.4 4.2 %all-to-all-start.1 = ((bf16[4,20,512]{2,1,0:T(8,128)(2,1)}), bf16[4,20,512]{2,1,0:T(8,128)(2,1)S(1)}, u32[]{:S(2)}, u32[]{:S(2)}) async-start(bf16[4,20,512]{2,1,0:T(8,128)(2,1)} %multiply_subtract_fusion), calls=%async_computation.1 | async-start | bytes 196608 | tf_op jit(solution)/shard_map/all_to_all | solution.py:282
  196.6 1.4 multiply_subtract_fusion.1
  198.1 3.5 %all-to-all-done.1 = bf16[4,20,512]{2,1,0:T(8,128)(2,1)S(1)} async-done(((bf16[4,20,512]{2,1,0:T(8,128)(2,1)}), bf16[4,20,512]{2,1,0:T(8,128)(2,1)S(1)}, u32[]{:S(2)}, u32[]{:S(2)}) %all-to-all-start.1) | async-done | bytes 81952 | tf_op jit(solution)/shard_map/all_to_all | solution.py:282
  205.5 3.0 fusion.13
  208.6 1.4 fusion.20
  210.0 1.4 fusion.68
  211.4 1.5 convolution_add_fusion
  212.9 1.3 copy-done
  214.9 1.3 reshape.251
  217.7 1.9 convolution_convert_fusion
  219.7 1.2 collective-permute-start.29
  225.2 3.7 %collective-permute-start.42 = (f32[96,80]{0,1:T(8,128)S(1)}, f32[96,80]{0,1:T(8,128)S(1)}, u32[]{:S(2)}, u32[]{:S(2)}) collective-permute-start(f32[96,80]{0,1:T(8,128)S(1)} %get-tuple-element.94), channel_id=1, source_target_pairs={{0,8},{2,10},{4,12},{6,14},{8,0},{10,2},{12,4},{14,6},{1,9},{3,11}... | collective-permute-start | bytes 92168 | tf_op jit(solution)/shard_map/ppermute | solution.py:68
  229.0 3.1 fusion.6
  234.7 2.3 collective-permute-done.44
  238.7 2.3 collective-permute-done.45
  247.9 1.5 collective-permute-start.18
  249.5 1.2 collective-permute-start.20
  250.8 9.5 %collective-permute-done.30 = bf16[2,4,48,768]{3,2,1,0:T(8,128)(2,1)S(1)} collective-permute-done((bf16[2,4,48,768]{3,2,1,0:T(8,128)(2,1)S(1)}, bf16[2,4,48,768]{3,2,1,0:T(8,128)(2,1)S(1)}, u32[]{:S(2)}, u32[]{:S(2)}) %collective-permute-start.30) | collective-permute-done | bytes 589856 | tf_op jit(solution)/shard_map/ppermute | solution.py:57
  262.7 10.2 %collective-permute-done.18 = bf16[2,4,48,768]{3,2,1,0:T(8,128)(2,1)S(1)} collective-permute-done((bf16[2,4,48,768]{3,2,1,0:T(8,128)(2,1)S(1)}, bf16[2,4,48,768]{3,2,1,0:T(8,128)(2,1)S(1)}, u32[]{:S(2)}, u32[]{:S(2)}) %collective-permute-start.18) | collective-permute-done | bytes 589856 | tf_op jit(solution)/shard_map/ppermute | solution.py:57
  275.3 4.7 %collective-permute-done.31 = bf16[2,4,48,384]{3,2,1,0:T(8,128)(2,1)S(1)} collective-permute-done((bf16[2,4,48,384]{3,2,1,0:T(8,128)(2,1)S(1)}, bf16[2,4,48,384]{3,2,1,0:T(8,128)(2,1)S(1)}, u32[]{:S(2)}, u32[]{:S(2)}) %collective-permute-start.31) | collective-permute-done | bytes 294944 | tf_op jit(solution)/shard_map/ppermute | solution.py:57
  280.2 1.2 collective-permute-start.34
  281.4 1.8 collective-permute-start.35
  284.3 1.2 collective-permute-start.22
  285.5 2.9 collective-permute-start.23
  288.4 3.5 %collective-permute-done.34 = bf16[2,2,48,384]{3,2,1,0:T(8,128)(2,1)S(1)} collective-permute-done((bf16[2,2,48,384]{3,2,1,0:T(8,128)(2,1)S(1)}, bf16[2,2,48,384]{3,2,1,0:T(8,128)(2,1)S(1)}, u32[]{:S(2)}, u32[]{:S(2)}) %collective-permute-start.34) | collective-permute-done | bytes 147488 | tf_op jit(solution)/shard_map/ppermute | solution.py:68
  291.9 5.4 %collective-permute-done.35 = bf16[2,2,48,384]{3,2,1,0:T(8,128)(2,1)S(1)} collective-permute-done((bf16[2,2,48,384]{3,2,1,0:T(8,128)(2,1)S(1)}, bf16[2,2,48,384]{3,2,1,0:T(8,128)(2,1)S(1)}, u32[]{:S(2)}, u32[]{:S(2)}) %collective-permute-start.35) | collective-permute-done | bytes 147488 | tf_op jit(solution)/shard_map/ppermute | solution.py:68
  297.3 2.3 collective-permute-done.36
  299.6 1.8 collective-permute-start.37
  301.4 1.6 collective-permute-start.38
  303.2 1.8 collective-permute-start.25
  305.0 1.6 collective-permute-start.26
  306.6 2.5 collective-permute-start.27
  309.2 1.3 collective-permute-done.39
  311.0 1.4 collective-permute-done.26
  312.4 1.2 collective-permute-done.27
  (294 shorter events, 54.5 us)
Async XLA Ops:
  7.2 34.8 %all-gather.9.cloned.1.call-start = ((), (), s32[]{:S(2)}) async-start(), calls=%async_computation.2 | async-start | bytes 2654208 | tf_op jit(solution)/shard_map/all_gather | solution.py:238
  9.3 66.8 %all-gather.11.cloned.1.call-start = ((), (), s32[]{:S(2)}) async-start(), calls=%async_computation.3 | async-start | bytes 2654208 | tf_op jit(solution)/shard_map/all_gather | solution.py:239
  10.2 98.9 %all-gather.13.cloned.1.call-start = ((), (), s32[]{:S(2)}) async-start(), calls=%async_computation.4 | async-start | bytes 2654208 | tf_op jit(solution)/shard_map/all_gather | solution.py:238
  11.0 130.4 %all-gather.15.cloned.1.call-start = ((), (), s32[]{:S(2)}) async-start(), calls=%async_computation.5 | async-start | bytes 2654208 | tf_op jit(solution)/shard_map/all_gather | solution.py:239
  11.0 3.3 %collective-permute-start.4 = (bf16[96,80]{0,1:T(8,128)(2,1)S(1)}, bf16[96,80]{0,1:T(8,128)(2,1)S(1)}, u32[]{:S(2)}, u32[]{:S(2)}) collective-permute-start(bf16[96,80]{0,1:T(8,128)(2,1)S(1)} %copy-done.29), channel_id=1, source_target_pairs={{0,2},{2,0},{4,6},{6,4},{8,10},{10,8},{12,14},{14,12},{1,3},{3,1},... | collective-permute-start | bytes 46088 | tf_op jit(solution)/shard_map/ppermute | solution.py:61
  11.8 15.8 %collective-permute-start = (bf16[32,768]{1,0:T(8,128)(2,1)S(1)}, bf16[32,768]{1,0:T(8,128)(2,1)S(1)}, u32[]{:S(2)}, u32[]{:S(2)}) collective-permute-start(bf16[32,768]{1,0:T(8,128)(2,1)S(1)} %get-tuple-element.68), channel_id=1, source_target_pairs={{0,2},{2,4},{4,6},{6,8},{8,10},{10,12},{12,14},{14,0},{1,3},{3,5},... | collective-permute-start | bytes 147464 | tf_op jit(solution)/shard_map/ppermute | solution.py:25
  12.3 15.2 %collective-permute-start.1 = (bf16[32,768]{1,0:T(8,128)(2,1)S(1)}, bf16[32,768]{1,0:T(8,128)(2,1)S(1)}, u32[]{:S(2)}, u32[]{:S(2)}) collective-permute-start(bf16[32,768]{1,0:T(8,128)(2,1)S(1)} %get-tuple-element.69), channel_id=1, source_target_pairs={{2,0},{4,2},{6,4},{8,6},{10,8},{12,10},{14,12},{0,14},{3,1},{5,3},... | collective-permute-start | bytes 147464 | tf_op jit(solution)/shard_map/ppermute | solution.py:27
  13.7 69.8 %copy-start.38 = (s32[512,1]{0,1:T(1,128)}, s32[512,1]{0,1:T(1,128)S(1)}, u32[]{:S(2)}) copy-start(s32[512,1]{0,1:T(1,128)S(1)} %get-tuple-element.119) | copy-start | bytes 6148
  13.7 69.8 %copy-start.40 = (s32[512,1]{0,1:T(1,128)}, s32[512,1]{0,1:T(1,128)S(1)}, u32[]{:S(2)}) copy-start(s32[512,1]{0,1:T(1,128)S(1)} %get-tuple-element.120) | copy-start | bytes 6148
  13.7 69.8 %copy-start.42 = (s32[512,1]{0,1:T(1,128)}, s32[512,1]{0,1:T(1,128)S(1)}, u32[]{:S(2)}) copy-start(s32[512,1]{0,1:T(1,128)S(1)} %get-tuple-element.121) | copy-start | bytes 6148
  13.7 69.8 %copy-start.44 = (s32[512,1]{0,1:T(1,128)}, s32[512,1]{0,1:T(1,128)S(1)}, u32[]{:S(2)}) copy-start(s32[512,1]{0,1:T(1,128)S(1)} %get-tuple-element.122) | copy-start | bytes 6148
  14.4 13.0 %collective-permute-start.5 = (bf16[192,80]{0,1:T(8,128)(2,1)S(1)}, bf16[192,80]{0,1:T(8,128)(2,1)S(1)}, u32[]{:S(2)}, u32[]{:S(2)}) collective-permute-start(bf16[192,80]{0,1:T(8,128)(2,1)S(1)} %get-tuple-element.116), channel_id=1, source_target_pairs={{0,4},{2,6},{4,8},{6,10},{8,12},{10,14},{12,0},{14,2},{1,5},{3,7},... | collective-permute-start | bytes 92168 | tf_op jit(solution)/shard_map/ppermute | solution.py:68
  16.1 11.4 %collective-permute-start.6 = (bf16[192,80]{0,1:T(8,128)(2,1)S(1)}, bf16[192,80]{0,1:T(8,128)(2,1)S(1)}, u32[]{:S(2)}, u32[]{:S(2)}) collective-permute-start(bf16[192,80]{0,1:T(8,128)(2,1)S(1)} %get-tuple-element.116), channel_id=1, source_target_pairs={{0,8},{2,10},{4,12},{6,14},{8,0},{10,2},{12,4},{14,6},{1,9},{3,11}... | collective-permute-start | bytes 92168 | tf_op jit(solution)/shard_map/ppermute | solution.py:68
  19.3 8.2 %collective-permute-start.7 = (bf16[192,80]{0,1:T(8,128)(2,1)S(1)}, bf16[192,80]{0,1:T(8,128)(2,1)S(1)}, u32[]{:S(2)}, u32[]{:S(2)}) collective-permute-start(bf16[192,80]{0,1:T(8,128)(2,1)S(1)} %get-tuple-element.116), channel_id=1, source_target_pairs={{0,12},{2,14},{4,0},{6,2},{8,4},{10,6},{12,8},{14,10},{1,13},{3,15... | collective-permute-start | bytes 92168 | tf_op jit(solution)/shard_map/ppermute | solution.py:68
  19.3 64.2 %copy-start.36 = (s32[512]{0:T(512)}, s32[512]{0:T(512)S(1)}, u32[]{:S(2)}) copy-start(s32[512]{0:T(512)S(1)} %iota_add_fusion.1) | copy-start | bytes 6148
  79.8 61.6 %copy-start.2 = (f32[512,768]{1,0:T(8,128)}, f32[512,768]{1,0:T(8,128)S(1)}, u32[]{:S(2)}) copy-start(f32[512,768]{1,0:T(8,128)S(1)} %get-tuple-element.130) | copy-start | bytes 4718596
  79.9 3.6 %collective-permute-start.2 = (bf16[32,768]{1,0:T(8,128)(2,1)S(1)}, bf16[32,768]{1,0:T(8,128)(2,1)S(1)}, u32[]{:S(2)}, u32[]{:S(2)}) collective-permute-start(bf16[32,768]{1,0:T(8,128)(2,1)S(1)} %get-tuple-element.66), channel_id=1, source_target_pairs={{0,2},{2,4},{4,6},{6,8},{8,10},{10,12},{12,14},{14,0},{1,3},{3,5},... | collective-permute-start | bytes 147464 | tf_op jit(solution)/shard_map/ppermute | solution.py:25
  80.3 3.2 collective-permute-start.3
  81.8 63.3 %copy-start.21 = (bf16[192,80]{0,1:T(8,128)(2,1)}, bf16[192,80]{0,1:T(8,128)(2,1)S(1)}, u32[]{:S(2)}) copy-start(bf16[192,80]{0,1:T(8,128)(2,1)S(1)} %get-tuple-element.95) | copy-start | bytes 92164
  81.8 63.3 %copy-start.23 = (bf16[192,80]{0,1:T(8,128)(2,1)}, bf16[192,80]{0,1:T(8,128)(2,1)S(1)}, u32[]{:S(2)}) copy-start(bf16[192,80]{0,1:T(8,128)(2,1)S(1)} %get-tuple-element.96) | copy-start | bytes 92164
  81.8 63.3 %copy-start.25 = (bf16[192,80]{0,1:T(8,128)(2,1)}, bf16[192,80]{0,1:T(8,128)(2,1)S(1)}, u32[]{:S(2)}) copy-start(bf16[192,80]{0,1:T(8,128)(2,1)S(1)} %get-tuple-element.97) | copy-start | bytes 92164
  81.8 63.3 %copy-start.27 = (bf16[192,80]{0,1:T(8,128)(2,1)}, bf16[192,80]{0,1:T(8,128)(2,1)S(1)}, u32[]{:S(2)}) copy-start(bf16[192,80]{0,1:T(8,128)(2,1)S(1)} %get-tuple-element.98) | copy-start | bytes 92164
  85.0 29.7 %copy-start.15 = (bf16[512,768]{1,0:T(8,128)(2,1)}, bf16[512,768]{1,0:T(8,128)(2,1)S(1)}, u32[]{:S(2)}) copy-start(bf16[512,768]{1,0:T(8,128)(2,1)S(1)} %convolution_convert_fusion.4) | copy-start | bytes 2359300
  145.1 19.2 %copy-start.14 = (bf16[512,768]{1,0:T(8,128)(2,1)S(1)}, bf16[512,768]{1,0:T(8,128)(2,1)}, u32[]{:S(2)}) copy-start(bf16[512,768]{1,0:T(8,128)(2,1)} %copy-done.13) | copy-start | bytes 2359300
  146.4 1.1 collective-permute-start.8
  148.2 3.5 %collective-permute-start.9 = (f32[14]{0:T(128)S(1)}, f32[14]{0:T(128)S(1)}, u32[]{:S(2)}, u32[]{:S(2)}) collective-permute-start(f32[14]{0:T(128)S(1)} %fusion.167), channel_id=1, source_target_pairs={{0,4},{2,6},{4,0},{6,2},{8,12},{10,14},{12,8},{14,10},{1,5},{3,7},... | collective-permute-start | bytes 176 | tf_op jit(solution)/shard_map/ppermute | solution.py:77
  151.8 4.4 %collective-permute-start.10 = (f32[14]{0:T(128)S(1)}, f32[14]{0:T(128)S(1)}, u32[]{:S(2)}, u32[]{:S(2)}) collective-permute-start(f32[14]{0:T(128)S(1)} %add.422), channel_id=1, source_target_pairs={{0,8},{2,10},{4,12},{6,14},{8,0},{10,2},{12,4},{14,6},{1,9},{3,11}... | collective-permute-start | bytes 176 | tf_op jit(solution)/shard_map/ppermute | solution.py:77
  159.3 10.4 %all-to-all-start = ((f32[1,80,512]{2,0,1:T(1,128)}), f32[1,80,512]{2,0,1:T(1,128)S(1)}, u32[]{:S(2)}, u32[]{:S(2)}) async-start(f32[1,80,512]{2,0,1:T(1,128)} %copy.39), calls=%async_computation | async-start | bytes 327680 | tf_op jit(solution)/shard_map/all_to_all | solution.py:268
  177.6 4.6 %collective-permute-start.11 = (f32[4,20]{1,0:T(4,128)S(1)}, f32[4,20]{1,0:T(4,128)}, u32[]{:S(2)}, u32[]{:S(2)}) collective-permute-start(f32[4,20]{1,0:T(4,128)S(1)} %reduce_sum.116), channel_id=1, source_target_pairs={{0,2},{2,0},{4,6},{6,4},{8,10},{10,8},{12,14},{14,12},{1,3},{3,1},... | collective-permute-start | bytes 968 | tf_op jit(solution)/shard_map/ppermute | solution.py:77
  182.9 3.6 %collective-permute-start.12 = (f32[4,20]{1,0:T(4,128)S(1)}, f32[4,20]{1,0:T(4,128)S(1)}, u32[]{:S(2)}, u32[]{:S(2)}) collective-permute-start(f32[4,20]{1,0:T(4,128)S(1)} %add.432), channel_id=1, source_target_pairs={{0,4},{2,6},{4,0},{6,2},{8,12},{10,14},{12,8},{14,10},{1,5},{3,7},... | collective-permute-start | bytes 968 | tf_op jit(solution)/shard_map/ppermute | solution.py:77
  186.5 4.5 %collective-permute-start.13 = (f32[4,20]{1,0:T(4,128)S(1)}, f32[4,20]{1,0:T(4,128)S(1)}, u32[]{:S(2)}, u32[]{:S(2)}) collective-permute-start(f32[4,20]{1,0:T(4,128)S(1)} %add.433), channel_id=1, source_target_pairs={{0,8},{2,10},{4,12},{6,14},{8,0},{10,2},{12,4},{14,6},{1,9},{3,11}... | collective-permute-start | bytes 968 | tf_op jit(solution)/shard_map/ppermute | solution.py:77
  192.4 9.1 %all-to-all-start.1 = ((bf16[4,20,512]{2,1,0:T(8,128)(2,1)}), bf16[4,20,512]{2,1,0:T(8,128)(2,1)S(1)}, u32[]{:S(2)}, u32[]{:S(2)}) async-start(bf16[4,20,512]{2,1,0:T(8,128)(2,1)} %multiply_subtract_fusion), calls=%async_computation.1 | async-start | bytes 196608 | tf_op jit(solution)/shard_map/all_to_all | solution.py:282
  216.5 7.6 %collective-permute-start.40 = (f32[4,96,80]{1,2,0:T(8,128)S(1)}, f32[4,96,80]{1,2,0:T(8,128)S(1)}, u32[]{:S(2)}, u32[]{:S(2)}) collective-permute-start(f32[4,96,80]{1,2,0:T(8,128)S(1)} %bitcast.261), channel_id=1, source_target_pairs={{0,2},{2,0},{4,6},{6,4},{8,10},{10,8},{12,14},{14,12},{1,3},{3,1},... | collective-permute-start | bytes 368648 | tf_op jit(solution)/shard_map/ppermute | solution.py:61
  216.6 5.2 %collective-permute-start.14 = (f32[32,768]{1,0:T(8,128)}, f32[32,768]{1,0:T(8,128)S(1)}, u32[]{:S(2)}, u32[]{:S(2)}) collective-permute-start(f32[32,768]{1,0:T(8,128)} %get-tuple-element.51), channel_id=1, source_target_pairs={{2,0},{4,2},{6,4},{8,6},{10,8},{12,10},{14,12},{0,14},{3,1},{5,3},... | collective-permute-start | bytes 294920 | tf_op jit(solution)/shard_map/ppermute | solution.py:37
  217.7 5.2 %collective-permute-start.15 = (f32[32,768]{1,0:T(8,128)}, f32[32,768]{1,0:T(8,128)S(1)}, u32[]{:S(2)}, u32[]{:S(2)}) collective-permute-start(f32[32,768]{1,0:T(8,128)} %get-tuple-element.50), channel_id=1, source_target_pairs={{14,0},{0,2},{2,4},{4,6},{6,8},{8,10},{10,12},{12,14},{15,1},{1,3}... | collective-permute-start | bytes 294920 | tf_op jit(solution)/shard_map/ppermute | solution.py:37
  219.7 22.8 %collective-permute-start.29 = (bf16[384,1536]{1,0:T(8,128)(2,1)S(1)}, bf16[384,1536]{1,0:T(8,128)(2,1)S(1)}, u32[]{:S(2)}, u32[]{:S(2)}) collective-permute-start(bf16[384,1536]{1,0:T(8,128)(2,1)S(1)} %convolution_convert_fusion), channel_id=1, source_target_pairs={{0,2},{2,0},{4,6},{6,4},{8,10},{10,8},{12,14},{14,12},{1,3},{3,1},... | collective-permute-start | bytes 3538952 | tf_op jit(solution)/shard_map/ppermute | solution.py:61
  221.7 20.0 %collective-permute-start.28 = (bf16[768,768]{1,0:T(8,128)(2,1)S(1)}, bf16[768,768]{1,0:T(8,128)(2,1)S(1)}, u32[]{:S(2)}, u32[]{:S(2)}) collective-permute-start(bf16[768,768]{1,0:T(8,128)(2,1)S(1)} %convolution_convert_fusion.2), channel_id=1, source_target_pairs={{0,2},{2,0},{4,6},{6,4},{8,10},{10,8},{12,14},{14,12},{1,3},{3,1},... | collective-permute-start | bytes 3538952 | tf_op jit(solution)/shard_map/ppermute | solution.py:61
  224.2 7.9 %collective-permute-start.41 = (f32[96,80]{0,1:T(8,128)S(1)}, f32[96,80]{0,1:T(8,128)S(1)}, u32[]{:S(2)}, u32[]{:S(2)}) collective-permute-start(f32[96,80]{0,1:T(8,128)S(1)} %get-tuple-element.92), channel_id=1, source_target_pairs={{0,4},{2,6},{4,8},{6,10},{8,12},{10,14},{12,0},{14,2},{1,5},{3,7},... | collective-permute-start | bytes 92168 | tf_op jit(solution)/shard_map/ppermute | solution.py:68
  225.2 6.9 %collective-permute-start.42 = (f32[96,80]{0,1:T(8,128)S(1)}, f32[96,80]{0,1:T(8,128)S(1)}, u32[]{:S(2)}, u32[]{:S(2)}) collective-permute-start(f32[96,80]{0,1:T(8,128)S(1)} %get-tuple-element.94), channel_id=1, source_target_pairs={{0,8},{2,10},{4,12},{6,14},{8,0},{10,2},{12,4},{14,6},{1,9},{3,11}... | collective-permute-start | bytes 92168 | tf_op jit(solution)/shard_map/ppermute | solution.py:68
  228.9 4.0 %collective-permute-start.43 = (f32[96,80]{0,1:T(8,128)S(1)}, f32[96,80]{0,1:T(8,128)S(1)}, u32[]{:S(2)}, u32[]{:S(2)}) collective-permute-start(f32[96,80]{0,1:T(8,128)S(1)} %get-tuple-element.93), channel_id=1, source_target_pairs={{0,12},{2,14},{4,0},{6,2},{8,4},{10,6},{12,8},{14,10},{1,13},{3,15... | collective-permute-start | bytes 92168 | tf_op jit(solution)/shard_map/ppermute | solution.py:68
  232.9 4.1 %collective-permute-start.44 = (f32[96,80]{0,1:T(8,128)S(1)}, f32[96,80]{0,1:T(8,128)S(1)}, u32[]{:S(2)}, u32[]{:S(2)}) collective-permute-start(f32[96,80]{0,1:T(8,128)S(1)} %fusion.108), channel_id=1, source_target_pairs={{0,16},{16,0},{1,17},{17,1},{2,18},{18,2},{3,19},{19,3},{4,20},{20... | collective-permute-start | bytes 92168 | tf_op jit(solution)/shard_map/ppermute | solution.py:57
  234.6 10.9 %collective-permute-start.17 = (bf16[384,1536]{1,0:T(8,128)(2,1)S(1)}, bf16[384,1536]{1,0:T(8,128)(2,1)S(1)}, u32[]{:S(2)}, u32[]{:S(2)}) collective-permute-start(bf16[384,1536]{1,0:T(8,128)(2,1)S(1)} %convolution_convert_fusion.1), channel_id=1, source_target_pairs={{0,2},{2,0},{4,6},{6,4},{8,10},{10,8},{12,14},{14,12},{1,3},{3,1},... | collective-permute-start | bytes 3538952 | tf_op jit(solution)/shard_map/ppermute | solution.py:61
  237.0 4.0 %collective-permute-start.45 = (f32[96,80]{0,1:T(8,128)S(1)}, f32[96,80]{0,1:T(8,128)S(1)}, u32[]{:S(2)}, u32[]{:S(2)}) collective-permute-start(f32[96,80]{0,1:T(8,128)S(1)} %add.480), channel_id=1, source_target_pairs={{0,1},{1,0},{2,3},{3,2},{4,5},{5,4},{6,7},{7,6},{8,9},{9,8},{10,11... | collective-permute-start | bytes 92168 | tf_op jit(solution)/shard_map/ppermute | solution.py:57
  238.6 7.7 %collective-permute-start.16 = (bf16[768,768]{1,0:T(8,128)(2,1)S(1)}, bf16[768,768]{1,0:T(8,128)(2,1)S(1)}, u32[]{:S(2)}, u32[]{:S(2)}) collective-permute-start(bf16[768,768]{1,0:T(8,128)(2,1)S(1)} %convolution_convert_fusion.3), channel_id=1, source_target_pairs={{0,2},{2,0},{4,6},{6,4},{8,10},{10,8},{12,14},{14,12},{1,3},{3,1},... | collective-permute-start | bytes 3538952 | tf_op jit(solution)/shard_map/ppermute | solution.py:61
  243.9 16.3 %collective-permute-start.30 = (bf16[2,4,48,768]{3,2,1,0:T(8,128)(2,1)S(1)}, bf16[2,4,48,768]{3,2,1,0:T(8,128)(2,1)S(1)}, u32[]{:S(2)}, u32[]{:S(2)}) collective-permute-start(bf16[2,4,48,768]{3,2,1,0:T(8,128)(2,1)S(1)} %fusion.46), channel_id=1, source_target_pairs={{0,16},{16,0},{1,17},{17,1},{2,18},{18,2},{3,19},{19,3},{4,20},{20... | collective-permute-start | bytes 1769480 | tf_op jit(solution)/shard_map/ppermute | solution.py:57
  244.9 16.5 %collective-permute-start.32 = (bf16[2,4,48,768]{3,2,0,1:T(8,128)(2,1)S(1)}, bf16[2,4,48,768]{3,2,0,1:T(8,128)(2,1)S(1)}, u32[]{:S(2)}, u32[]{:S(2)}) collective-permute-start(bf16[2,4,48,768]{3,2,0,1:T(8,128)(2,1)S(1)} %fusion.42), channel_id=1, source_target_pairs={{0,1},{1,0},{2,3},{3,2},{4,5},{5,4},{6,7},{7,6},{8,9},{9,8},{10,11... | collective-permute-start | bytes 1769480 | tf_op jit(solution)/shard_map/ppermute | solution.py:57
  247.9 25.0 %collective-permute-start.18 = (bf16[2,4,48,768]{3,2,1,0:T(8,128)(2,1)S(1)}, bf16[2,4,48,768]{3,2,1,0:T(8,128)(2,1)S(1)}, u32[]{:S(2)}, u32[]{:S(2)}) collective-permute-start(bf16[2,4,48,768]{3,2,1,0:T(8,128)(2,1)S(1)} %fusion.54), channel_id=1, source_target_pairs={{0,16},{16,0},{1,17},{17,1},{2,18},{18,2},{3,19},{19,3},{4,20},{20... | collective-permute-start | bytes 1769480 | tf_op jit(solution)/shard_map/ppermute | solution.py:57
  249.5 24.5 %collective-permute-start.20 = (bf16[2,4,48,768]{3,2,0,1:T(8,128)(2,1)S(1)}, bf16[2,4,48,768]{3,2,0,1:T(8,128)(2,1)S(1)}, u32[]{:S(2)}, u32[]{:S(2)}) collective-permute-start(bf16[2,4,48,768]{3,2,0,1:T(8,128)(2,1)S(1)} %fusion.50), channel_id=1, source_target_pairs={{0,1},{1,0},{2,3},{3,2},{4,5},{5,4},{6,7},{7,6},{8,9},{9,8},{10,11... | collective-permute-start | bytes 1769480 | tf_op jit(solution)/shard_map/ppermute | solution.py:57
  260.4 19.5 %collective-permute-start.31 = (bf16[2,4,48,384]{3,2,1,0:T(8,128)(2,1)S(1)}, bf16[2,4,48,384]{3,2,1,0:T(8,128)(2,1)S(1)}, u32[]{:S(2)}, u32[]{:S(2)}) collective-permute-start(bf16[2,4,48,384]{3,2,1,0:T(8,128)(2,1)S(1)} %dynamic-slice_convert_fusion.1), channel_id=1, source_target_pairs={{0,1},{1,0},{2,3},{3,2},{4,5},{5,4},{6,7},{7,6},{8,9},{9,8},{10,11... | collective-permute-start | bytes 884744 | tf_op jit(solution)/shard_map/ppermute | solution.py:57
  261.5 18.5 %collective-permute-start.33 = (bf16[2,4,48,384]{3,2,0,1:T(8,128)(2,1)S(1)}, bf16[2,4,48,384]{3,2,0,1:T(8,128)(2,1)S(1)}, u32[]{:S(2)}, u32[]{:S(2)}) collective-permute-start(bf16[2,4,48,384]{3,2,0,1:T(8,128)(2,1)S(1)} %dynamic-slice_convert_fusion), channel_id=1, source_target_pairs={{0,16},{16,0},{1,17},{17,1},{2,18},{18,2},{3,19},{19,3},{4,20},{20... | collective-permute-start | bytes 884744 | tf_op jit(solution)/shard_map/ppermute | solution.py:57
  273.1 11.0 %collective-permute-start.19 = (bf16[2,4,48,384]{3,2,1,0:T(8,128)(2,1)S(1)}, bf16[2,4,48,384]{3,2,1,0:T(8,128)(2,1)S(1)}, u32[]{:S(2)}, u32[]{:S(2)}) collective-permute-start(bf16[2,4,48,384]{3,2,1,0:T(8,128)(2,1)S(1)} %dynamic-slice_convert_fusion.3), channel_id=1, source_target_pairs={{0,1},{1,0},{2,3},{3,2},{4,5},{5,4},{6,7},{7,6},{8,9},{9,8},{10,11... | collective-permute-start | bytes 884744 | tf_op jit(solution)/shard_map/ppermute | solution.py:57
  274.2 9.9 %collective-permute-start.21 = (bf16[2,4,48,384]{3,2,0,1:T(8,128)(2,1)S(1)}, bf16[2,4,48,384]{3,2,0,1:T(8,128)(2,1)S(1)}, u32[]{:S(2)}, u32[]{:S(2)}) collective-permute-start(bf16[2,4,48,384]{3,2,0,1:T(8,128)(2,1)S(1)} %dynamic-slice_convert_fusion.2), channel_id=1, source_target_pairs={{0,16},{16,0},{1,17},{17,1},{2,18},{18,2},{3,19},{19,3},{4,20},{20... | collective-permute-start | bytes 884744 | tf_op jit(solution)/shard_map/ppermute | solution.py:57
  280.2 11.7 %collective-permute-start.34 = (bf16[2,2,48,384]{3,2,1,0:T(8,128)(2,1)S(1)}, bf16[2,2,48,384]{3,2,1,0:T(8,128)(2,1)S(1)}, u32[]{:S(2)}, u32[]{:S(2)}) collective-permute-start(bf16[2,2,48,384]{3,2,1,0:T(8,128)(2,1)S(1)} %get-tuple-element.59), channel_id=1, source_target_pairs={{0,4},{2,6},{4,8},{6,10},{8,12},{10,14},{12,0},{14,2},{1,5},{3,7},... | collective-permute-start | bytes 442376 | tf_op jit(solution)/shard_map/ppermute | solution.py:68
  281.4 15.9 %collective-permute-start.35 = (bf16[2,2,48,384]{3,2,1,0:T(8,128)(2,1)S(1)}, bf16[2,2,48,384]{3,2,1,0:T(8,128)(2,1)S(1)}, u32[]{:S(2)}, u32[]{:S(2)}) collective-permute-start(bf16[2,2,48,384]{3,2,1,0:T(8,128)(2,1)S(1)} %get-tuple-element.60), channel_id=1, source_target_pairs={{0,8},{2,10},{4,12},{6,14},{8,0},{10,2},{12,4},{14,6},{1,9},{3,11}... | collective-permute-start | bytes 442376 | tf_op jit(solution)/shard_map/ppermute | solution.py:68
  283.2 16.3 %collective-permute-start.36 = (bf16[2,2,48,384]{3,2,1,0:T(8,128)(2,1)S(1)}, bf16[2,2,48,384]{3,2,1,0:T(8,128)(2,1)S(1)}, u32[]{:S(2)}, u32[]{:S(2)}) collective-permute-start(bf16[2,2,48,384]{3,2,1,0:T(8,128)(2,1)S(1)} %get-tuple-element.61), channel_id=1, source_target_pairs={{0,12},{2,14},{4,0},{6,2},{8,4},{10,6},{12,8},{14,10},{1,13},{3,15... | collective-permute-start | bytes 442376 | tf_op jit(solution)/shard_map/ppermute | solution.py:68
  284.3 18.6 %collective-permute-start.22 = (bf16[2,2,48,384]{3,2,1,0:T(8,128)(2,1)S(1)}, bf16[2,2,48,384]{3,2,1,0:T(8,128)(2,1)S(1)}, u32[]{:S(2)}, u32[]{:S(2)}) collective-permute-start(bf16[2,2,48,384]{3,2,1,0:T(8,128)(2,1)S(1)} %get-tuple-element.56), channel_id=1, source_target_pairs={{0,4},{2,6},{4,8},{6,10},{8,12},{10,14},{12,0},{14,2},{1,5},{3,7},... | collective-permute-start | bytes 442376 | tf_op jit(solution)/shard_map/ppermute | solution.py:68
  285.5 17.7 %collective-permute-start.23 = (bf16[2,2,48,384]{3,2,1,0:T(8,128)(2,1)S(1)}, bf16[2,2,48,384]{3,2,1,0:T(8,128)(2,1)S(1)}, u32[]{:S(2)}, u32[]{:S(2)}) collective-permute-start(bf16[2,2,48,384]{3,2,1,0:T(8,128)(2,1)S(1)} %get-tuple-element.57), channel_id=1, source_target_pairs={{0,8},{2,10},{4,12},{6,14},{8,0},{10,2},{12,4},{14,6},{1,9},{3,11}... | collective-permute-start | bytes 442376 | tf_op jit(solution)/shard_map/ppermute | solution.py:68
  291.9 11.3 %collective-permute-start.24 = (bf16[2,2,48,384]{3,2,1,0:T(8,128)(2,1)S(1)}, bf16[2,2,48,384]{3,2,1,0:T(8,128)(2,1)S(1)}, u32[]{:S(2)}, u32[]{:S(2)}) collective-permute-start(bf16[2,2,48,384]{3,2,1,0:T(8,128)(2,1)S(1)} %get-tuple-element.58), channel_id=1, source_target_pairs={{0,12},{2,14},{4,0},{6,2},{8,4},{10,6},{12,8},{14,10},{1,13},{3,15... | collective-permute-start | bytes 442376 | tf_op jit(solution)/shard_map/ppermute | solution.py:68
  299.6 7.0 %collective-permute-start.37 = (bf16[2,2,48,384]{3,2,1,0:T(8,128)(2,1)S(1)}, bf16[2,2,48,384]{3,2,1,0:T(8,128)(2,1)S(1)}, u32[]{:S(2)}, u32[]{:S(2)}) collective-permute-start(bf16[2,2,48,384]{3,2,1,0:T(8,128)(2,1)S(1)} %fusion.81), channel_id=1, source_target_pairs={{0,16},{1,17},{16,0},{17,1},{2,18},{3,19},{18,2},{19,3},{4,20},{5,... | collective-permute-start | bytes 442376 | tf_op jit(solution)/shard_map/ppermute | solution.py:179
  301.4 7.8 %collective-permute-start.38 = (bf16[2,2,48,384]{3,2,1,0:T(8,128)(2,1)S(1)}, bf16[2,2,48,384]{3,2,1,0:T(8,128)(2,1)S(1)}, u32[]{:S(2)}, u32[]{:S(2)}) collective-permute-start(bf16[2,2,48,384]{3,2,1,0:T(8,128)(2,1)S(1)} %fusion.81), channel_id=1, source_target_pairs={{0,1},{1,0},{16,17},{17,16},{2,3},{3,2},{18,19},{19,18},{4,5},{5,4... | collective-permute-start | bytes 442376 | tf_op jit(solution)/shard_map/ppermute | solution.py:179
  302.9 7.6 %collective-permute-start.39 = (bf16[2,2,48,384]{3,2,1,0:T(8,128)(2,1)S(1)}, bf16[2,2,48,384]{3,2,1,0:T(8,128)(2,1)S(1)}, u32[]{:S(2)}, u32[]{:S(2)}) collective-permute-start(bf16[2,2,48,384]{3,2,1,0:T(8,128)(2,1)S(1)} %fusion.81), channel_id=1, source_target_pairs={{0,17},{1,16},{16,1},{17,0},{2,19},{3,18},{18,3},{19,2},{4,21},{5,... | collective-permute-start | bytes 442376 | tf_op jit(solution)/shard_map/ppermute | solution.py:179
  303.2 7.8 %collective-permute-start.25 = (bf16[2,2,48,384]{3,2,1,0:T(8,128)(2,1)S(1)}, bf16[2,2,48,384]{3,2,1,0:T(8,128)(2,1)S(1)}, u32[]{:S(2)}, u32[]{:S(2)}) collective-permute-start(bf16[2,2,48,384]{3,2,1,0:T(8,128)(2,1)S(1)} %fusion.93), channel_id=1, source_target_pairs={{0,16},{1,17},{16,0},{17,1},{2,18},{3,19},{18,2},{19,3},{4,20},{5,... | collective-permute-start | bytes 442376 | tf_op jit(solution)/shard_map/ppermute | solution.py:179
  305.0 7.4 %collective-permute-start.26 = (bf16[2,2,48,384]{3,2,1,0:T(8,128)(2,1)S(1)}, bf16[2,2,48,384]{3,2,1,0:T(8,128)(2,1)S(1)}, u32[]{:S(2)}, u32[]{:S(2)}) collective-permute-start(bf16[2,2,48,384]{3,2,1,0:T(8,128)(2,1)S(1)} %fusion.93), channel_id=1, source_target_pairs={{0,1},{1,0},{16,17},{17,16},{2,3},{3,2},{18,19},{19,18},{4,5},{5,4... | collective-permute-start | bytes 442376 | tf_op jit(solution)/shard_map/ppermute | solution.py:179
  306.6 7.0 %collective-permute-start.27 = (bf16[2,2,48,384]{3,2,1,0:T(8,128)(2,1)S(1)}, bf16[2,2,48,384]{3,2,1,0:T(8,128)(2,1)S(1)}, u32[]{:S(2)}, u32[]{:S(2)}) collective-permute-start(bf16[2,2,48,384]{3,2,1,0:T(8,128)(2,1)S(1)} %fusion.93), channel_id=1, source_target_pairs={{0,17},{1,16},{16,1},{17,0},{2,19},{3,18},{18,3},{19,2},{4,21},{5,... | collective-permute-start | bytes 442376 | tf_op jit(solution)/shard_map/ppermute | solution.py:179
  (42 other events, 233.9 us)
Sparse Core Ops, SparseCore 0:
  9.7 32.3 all-gather.8
  43.7 32.3 all-gather.10
  78.3 30.7 all-gather.12
  110.6 30.7 all-gather.14

commit v2 on v1

--- a/solution.py
+++ b/solution.py
@@ -216,6 +216,37 @@
     return mine + swapped(mine, "grp")
 
 
+def gathered(block, dim):
+    if not paired():
+        return lax.all_gather(block, "tile", axis=0, tiled=True)
+    chips = lax.axis_size("tile") // 2
+    chip = lax.axis_index("tile") // 2
+    core = lax.axis_index("tile") % 2
+    x = lax.axis_index("member")
+    y = lax.axis_index("grp")
+    first, second = half(block, 0, dim), half(block, 1, dim)
+    mine = jnp.stack([half(first, x, dim), half(second, y, dim)])
+    columns = jnp.stack([mine] + [shifted(mine, k) for k in range(1, chips)], axis=1)
+
+    def joined(kept, axis, index):
+        got = swapped(kept, axis)
+        low = jnp.where(index == 0, kept, got)
+        high = jnp.where(index == 0, got, kept)
+        return [low, high]
+
+    chip_rows = jnp.concatenate(
+        joined(columns[0], "member", x) + joined(columns[1], "grp", y), axis=dim + 1
+    )
+    other = core_swapped(chip_rows)
+    order = [(chip - z) % chips for z in range(chips)]
+    pieces = []
+    for z in range(chips):
+        here, there = pick(chip_rows, order[z], 0), pick(other, order[z], 0)
+        pieces.append(jnp.where(core == 0, here, there))
+        pieces.append(jnp.where(core == 0, there, here))
+    return jnp.concatenate(pieces, axis=0)
+
+
 def gathered_out(block):
     chips = lax.axis_size("tile") // 2
     chip = lax.axis_index("tile") // 2
@@ -235,8 +266,8 @@
     row_ids = jnp.arange(nodes_dev, dtype=jnp.int32)
     global_rows = lax.axis_index("tile") * nodes_dev + row_ids
     local_index = (neighbours - global_rows[:, None] + HALO) % total_nodes + row_ids[:, None]
-    full_up = [lax.all_gather(w_up[l], "tile", axis=0, tiled=True) for l in range(LAYERS)]
-    full_down = [lax.all_gather(w_down[l], "tile", axis=0, tiled=True) for l in range(LAYERS)]
+    full_up = [gathered(w_up[l], 1) for l in range(LAYERS)]
+    full_down = [gathered(w_down[l], 0) for l in range(LAYERS)]
     full_out = gathered_out(w_out)
     matrix = blend_matrix(local_index, nodes_dev)
     hidden_state = latent.astype(jnp.float32) + noise[0].astype(jnp.float32)

time: 324 us -> 298 us (0.920); the launches traced: 323 us -> 293 us
  waiting for transfers between devices: 154 us -> 103 us
  starting transfers between devices: 56 us -> 94.3 us
  between operations: 22.6 us -> 10 us
  matrix products: 41 us -> 32.7 us
  other arithmetic: 19.4 us -> 26.1 us
    all_gather x4 -> x0, waiting for transfers between devices: 92.4 us -> none  [the longest x2 55.3 us: shards(): lax.all_gather(w_down[l], 'tile', axis=0, tiled=True)]
    ppermute x12 -> x24, starting transfers between devices: 17.7 us -> 40.8 us  [shifted(): return lax.ppermute(block, 'tile', route)]
    ppermute x10 -> x18, waiting for transfers between devices: 29 us -> 47.1 us  [swapped(): return lax.ppermute(block, axis, [(0, 1), (1, 0)])]
    ppermute x12 -> x24, waiting for transfers between devices: 11.9 us -> 27.6 us  [shifted(): return lax.ppermute(block, 'tile', route)]
    ppermute x10 -> x18, starting transfers between devices: 10.1 us -> 20.2 us  [swapped(): return lax.ppermute(block, axis, [(0, 1), (1, 0)])]
    ppermute x6, starting transfers between devices: 4.56 us -> 11.4 us  [tile_sum(): lax.ppermute(values, 'tile', [(i, i ^ step) for i in range(count)])]
    ppermute x6, waiting for transfers between devices: 10.8 us -> 5.17 us  [tile_sum(): lax.ppermute(values, 'tile', [(i, i ^ step) for i in range(count)])]
    ppermute x2, waiting for transfers between devices: 0.14 us -> 4.95 us  [passed_along(): return lax.ppermute(block, axis, route)]
  transfers between devices with their start and end apart: 52 -> 72, of which waited for: 25 -> 31; matrix products, arithmetic and copies ran while one was open for 15% -> 14% of each run, Pallas kernels for 0% -> 0%
where the time goes in v2:
time: 298 us; the launch traced here: 293 us
  waiting for transfers between devices  103 us (35%)
  starting transfers between devices  94.3 us (32%)
  matrix products  32.7 us (11%)
  local copies, waits for them, and re-layouts  27 us (9%)
  other arithmetic  26.1 us (9%)
  between operations  10 us (3%)
    ppermute x18, waiting for transfers between devices, swapped(): return lax.ppermute(block, axis, [(0, 1), (1, 0)])  47.1 us
    ppermute x24, starting transfers between devices, shifted(): return lax.ppermute(block, 'tile', route)  40.8 us
    ppermute x24, waiting for transfers between devices, shifted(): return lax.ppermute(block, 'tile', route)  27.6 us
    ppermute x18, starting transfers between devices, swapped(): return lax.ppermute(block, axis, [(0, 1), (1, 0)])  20.2 us
    ppermute x6, starting transfers between devices, tile_sum(): lax.ppermute(values, 'tile', [(i, i ^ step) for i in range(count)])  11.4 us
    ppermute x6, starting transfers between devices, from_corner(): return lax.ppermute(own, ('member', 'grp'), route)  8.14 us
    dot_general x8, matrix products, product(): return jnp.dot(chosen.T, right, preferred_element_type=jnp.float32)  7.5 us
    dot_general x2, matrix products, shards(): jnp.dot(blended, full_up[layer_index], preferred_element_type=jnp.float32)  6.97 us
  transfers between devices with their start and end apart: 72, of which 31 were waited for; matrix products, arithmetic and copies ran while one was open for 14% of the time, Pallas kernels for 0%

profile of v2, /device:TPU:8, one launch (start us, length us, event | category | flops | bytes accessed | tf_op | source)
XLA Modules:
  0.0 293.2 jit_solution(3429864896791334557)
XLA Ops:
  2.7 2.6 collective-permute-start.9
  9.2 2.8 collective-permute-start.30
  24.0 1.7 collective-permute-start.1
  25.9 3.5 %collective-permute-done = bf16[32,768]{1,0:T(8,128)(2,1)S(1)} collective-permute-done((bf16[32,768]{1,0:T(8,128)(2,1)S(1)}, bf16[32,768]{1,0:T(8,128)(2,1)S(1)}, u32[]{:S(2)}, u32[]{:S(2)}) %collective-permute-start) | collective-permute-done | bytes 49184 | tf_op jit(solution)/shard_map/ppermute | solution.py:25
  29.4 4.2 %collective-permute-start.22 = (bf16[2,48,768]{2,1,0:T(8,128)(2,1)}, bf16[2,48,768]{2,1,0:T(8,128)(2,1)S(1)}, u32[]{:S(2)}, u32[]{:S(2)}) collective-permute-start(bf16[2,48,768]{2,1,0:T(8,128)(2,1)} %get-tuple-element.154), channel_id=1, source_target_pairs={{0,4},{2,6},{4,8},{6,10},{8,12},{10,14},{12,0},{14,2},{1,5},{3,7},... | collective-permute-start | bytes 442376 | tf_op jit(solution)/shard_map/ppermute | solution.py:68
  35.0 2.2 collective-permute-start.10
  37.2 7.7 %collective-permute-done.22 = bf16[2,48,768]{2,1,0:T(8,128)(2,1)S(1)} collective-permute-done((bf16[2,48,768]{2,1,0:T(8,128)(2,1)}, bf16[2,48,768]{2,1,0:T(8,128)(2,1)S(1)}, u32[]{:S(2)}, u32[]{:S(2)}) %collective-permute-start.22) | collective-permute-done | bytes 147488 | tf_op jit(solution)/shard_map/ppermute | solution.py:68
  44.9 2.4 collective-permute-start.16
  47.5 3.8 %collective-permute-start.3 = (bf16[2,96,384]{2,1,0:T(8,128)(2,1)S(1)}, bf16[2,96,384]{2,1,0:T(8,128)(2,1)S(1)}, u32[]{:S(2)}, u32[]{:S(2)}) collective-permute-start(bf16[2,96,384]{2,1,0:T(8,128)(2,1)S(1)} %copy-done.33), channel_id=1, source_target_pairs={{0,8},{2,10},{4,12},{6,14},{8,0},{10,2},{12,4},{14,6},{1,9},{3,11}... | collective-permute-start | bytes 442376 | tf_op jit(solution)/shard_map/ppermute | solution.py:68
  51.4 2.0 collective-permute-start.4
  54.5 8.6 %collective-permute-done.3 = bf16[2,96,384]{2,1,0:T(8,128)(2,1)S(1)} collective-permute-done((bf16[2,96,384]{2,1,0:T(8,128)(2,1)S(1)}, bf16[2,96,384]{2,1,0:T(8,128)(2,1)S(1)}, u32[]{:S(2)}, u32[]{:S(2)}) %collective-permute-start.3) | collective-permute-done | bytes 147488 | tf_op jit(solution)/shard_map/ppermute | solution.py:68
  63.1 2.5 collective-permute-start.18
  65.6 1.5 collective-permute-start.25
  67.1 1.5 collective-permute-start.26
  71.6 3.9 %collective-permute-done.25 = bf16[4,48,768]{2,1,0:T(8,128)(2,1)S(1)} collective-permute-done((bf16[4,48,768]{2,1,0:T(8,128)(2,1)S(1)}, bf16[4,48,768]{2,1,0:T(8,128)(2,1)S(1)}, u32[]{:S(2)}, u32[]{:S(2)}) %collective-permute-start.25) | collective-permute-done | bytes 294944 | tf_op jit(solution)/shard_map/ppermute | solution.py:57
  75.5 1.5 collective-permute-start.6
  77.0 1.5 collective-permute-start.19
  78.7 9.4 %collective-permute-done.5 = bf16[4,96,384]{2,1,0:T(8,128)(2,1)S(1)} collective-permute-done((bf16[4,96,384]{2,1,0:T(8,128)(2,1)S(1)}, bf16[4,96,384]{2,1,0:T(8,128)(2,1)S(1)}, u32[]{:S(2)}, u32[]{:S(2)}) %collective-permute-start.5) | collective-permute-done | bytes 294944 | tf_op jit(solution)/shard_map/ppermute | solution.py:57
  88.1 1.5 collective-permute-start.20
  89.9 3.3 %collective-permute-done.19 = bf16[4,96,384]{2,1,0:T(8,128)(2,1)S(1)} collective-permute-done((bf16[4,96,384]{2,1,0:T(8,128)(2,1)S(1)}, bf16[4,96,384]{2,1,0:T(8,128)(2,1)S(1)}, u32[]{:S(2)}, u32[]{:S(2)}) %collective-permute-start.19) | collective-permute-done | bytes 294944 | tf_op jit(solution)/shard_map/ppermute | solution.py:57
  93.2 1.7 collective-permute-done.20
  98.8 3.5 %multiply_convert_fusion.1 = (bf16[512,1536]{1,0:T(8,128)(2,1)S(1)}, f32[512,1536]{1,0:T(8,128)}) fusion(bf16[512,768]{1,0:T(8,128)(2,1)S(1)} %convolution_convert_fusion.5, bf16[768,1536]{1,0:T(8,128)(2,1)S(1)} %bitcast_dynamic-update-slice_fusion.24), kind=kOutput, calls=%fused_computation.19 | convolution fusion | flops 1215037440 | bytes 7864320 | tf_op jit(solution)/shard_map/dot_general | solution.py:277
  103.1 1.5 multiply_reduce_fusion.3
  105.0 2.1 collective-permute-start.15
  110.3 3.5 %multiply_convert_fusion = (bf16[512,1536]{1,0:T(8,128)(2,1)S(1)}, f32[512,1536]{1,0:T(8,128)}) fusion(bf16[512,768]{1,0:T(8,128)(2,1)S(1)} %convolution_convert_fusion.4, bf16[768,1536]{1,0:T(8,128)(2,1)S(1)} %bitcast_dynamic-update-slice_fusion.8), kind=kOutput, calls=%fused_computation.18 | convolution fusion | flops 1215037440 | bytes 7864320 | tf_op jit(solution)/shard_map/dot_general | solution.py:277
  113.8 1.5 multiply_reduce_fusion.2
  117.2 2.1 collective-permute-start.32
  120.7 1.9 collective-permute-start.33
  124.3 4.1 %collective-permute-start.34 = (f32[14]{0:T(128)S(1)}, f32[14]{0:T(128)S(1)}, u32[]{:S(2)}, u32[]{:S(2)}) collective-permute-start(f32[14]{0:T(128)S(1)} %add.515), channel_id=1, source_target_pairs={{0,8},{2,10},{4,12},{6,14},{8,0},{10,2},{12,4},{14,6},{1,9},{3,11}... | collective-permute-start | bytes 176 | tf_op jit(solution)/shard_map/ppermute | solution.py:77
  128.4 1.7 copy.73
  133.2 3.7 %all-to-all-start = ((f32[1,80,512]{2,0,1:T(1,128)}), f32[1,80,512]{2,0,1:T(1,128)S(1)}, u32[]{:S(2)}, u32[]{:S(2)}) async-start(f32[1,80,512]{2,0,1:T(1,128)} %copy.71), calls=%async_computation | async-start | bytes 327680 | tf_op jit(solution)/shard_map/all_to_all | solution.py:299
  138.2 1.7 copy.78
  139.9 2.1 all-to-all-done
  144.1 1.9 fusion.48
  147.4 1.6 div.111
  154.4 2.3 collective-permute-done.36
  156.7 2.8 collective-permute-start.37
  159.5 1.7 collective-permute-done.37
  162.6 3.5 %all-to-all-start.1 = ((bf16[4,20,512]{2,1,0:T(8,128)(2,1)}), bf16[4,20,512]{2,1,0:T(8,128)(2,1)S(1)}, u32[]{:S(2)}, u32[]{:S(2)}) async-start(bf16[4,20,512]{2,1,0:T(8,128)(2,1)} %multiply_subtract_fusion), calls=%async_computation.1 | async-start | bytes 196608 | tf_op jit(solution)/shard_map/all_to_all | solution.py:313
  166.8 4.2 %all-to-all-done.1 = bf16[4,20,512]{2,1,0:T(8,128)(2,1)S(1)} async-done(((bf16[4,20,512]{2,1,0:T(8,128)(2,1)}), bf16[4,20,512]{2,1,0:T(8,128)(2,1)S(1)}, u32[]{:S(2)}, u32[]{:S(2)}) %all-to-all-start.1) | async-done | bytes 81952 | tf_op jit(solution)/shard_map/all_to_all | solution.py:313
  174.9 3.0 %fusion.13 = bf16[512,1536]{1,0:T(8,128)(2,1)S(1)} fusion(f32[512,1536]{1,0:T(8,128)S(1)} %copy-done.60, bf16[1536,768]{1,0:T(8,128)(2,1)S(1)} %copy-done.39, f32[512,768]{1,0:T(8,128)S(1)} %add_add_fusion.1), kind=kOutput, calls=%fused_computation.17 | convolution fusion | flops 1224081408 | bytes 8650752 | tf_op jit(solution)/shard_map/dot_general | solution.py:326
  183.7 2.0 reshape.327
  185.8 1.5 constant_dynamic-slice_fusion.1
  187.4 2.1 convolution_convert_fusion.2
  193.2 4.2 %collective-permute-done.39 = f32[32,768]{1,0:T(8,128)S(1)} collective-permute-done((f32[32,768]{1,0:T(8,128)S(1)}, f32[32,768]{1,0:T(8,128)S(1)}, u32[]{:S(2)}, u32[]{:S(2)}) %collective-permute-start.39) | collective-permute-done | bytes 98336 | tf_op jit(solution)/shard_map/ppermute | solution.py:37
  198.8 3.3 %collective-permute-start.67 = (f32[96,80]{0,1:T(8,128)S(1)}, f32[96,80]{0,1:T(8,128)S(1)}, u32[]{:S(2)}, u32[]{:S(2)}) collective-permute-start(f32[96,80]{0,1:T(8,128)S(1)} %get-tuple-element.131), channel_id=1, source_target_pairs={{0,12},{2,14},{4,0},{6,2},{8,4},{10,6},{12,8},{14,10},{1,13},{3,15... | collective-permute-start | bytes 92168 | tf_op jit(solution)/shard_map/ppermute | solution.py:68
  202.1 2.4 collective-permute-start.66
  204.5 3.0 %fusion.6 = bf16[512,1536]{1,0:T(8,128)(2,1)S(1)} fusion(f32[512,1536]{1,0:T(8,128)S(1)} %copy-done.59, bf16[512,768]{1,0:T(8,128)(2,1)S(1)} %fusion.16, bf16[1536,768]{1,0:T(8,128)(2,1)S(1)} %copy-done.37), kind=kOutput, calls=%fused_computation.10 | convolution fusion | flops 1223688192 | bytes 7864320 | tf_op jit(solution)/shard_map/dot_general | solution.py:326
  209.2 2.4 collective-permute-done.68
  213.8 1.8 collective-permute-done.69
  222.2 1.5 collective-permute-start.42
  225.1 9.5 %collective-permute-done.54 = bf16[2,4,48,768]{3,2,1,0:T(8,128)(2,1)S(1)} collective-permute-done((bf16[2,4,48,768]{3,2,1,0:T(8,128)(2,1)S(1)}, bf16[2,4,48,768]{3,2,1,0:T(8,128)(2,1)S(1)}, u32[]{:S(2)}, u32[]{:S(2)}) %collective-permute-start.54) | collective-permute-done | bytes 589856 | tf_op jit(solution)/shard_map/ppermute | solution.py:57
  237.0 10.2 %collective-permute-done.42 = bf16[2,4,48,768]{3,2,1,0:T(8,128)(2,1)S(1)} collective-permute-done((bf16[2,4,48,768]{3,2,1,0:T(8,128)(2,1)S(1)}, bf16[2,4,48,768]{3,2,1,0:T(8,128)(2,1)S(1)}, u32[]{:S(2)}, u32[]{:S(2)}) %collective-permute-start.42) | collective-permute-done | bytes 589856 | tf_op jit(solution)/shard_map/ppermute | solution.py:57
  249.7 4.7 %collective-permute-done.55 = bf16[2,4,48,384]{3,2,1,0:T(8,128)(2,1)S(1)} collective-permute-done((bf16[2,4,48,384]{3,2,1,0:T(8,128)(2,1)S(1)}, bf16[2,4,48,384]{3,2,1,0:T(8,128)(2,1)S(1)}, u32[]{:S(2)}, u32[]{:S(2)}) %collective-permute-start.55) | collective-permute-done | bytes 294944 | tf_op jit(solution)/shard_map/ppermute | solution.py:57
  254.6 2.9 collective-permute-start.58
  257.5 2.7 collective-permute-start.59
  260.5 2.1 collective-permute-start.46
  262.5 2.0 collective-permute-start.47
  264.5 3.2 %collective-permute-done.58 = bf16[2,2,48,384]{3,2,1,0:T(8,128)(2,1)S(1)} collective-permute-done((bf16[2,2,48,384]{3,2,1,0:T(8,128)(2,1)S(1)}, bf16[2,2,48,384]{3,2,1,0:T(8,128)(2,1)S(1)}, u32[]{:S(2)}, u32[]{:S(2)}) %collective-permute-start.58) | collective-permute-done | bytes 147488 | tf_op jit(solution)/shard_map/ppermute | solution.py:68
  267.8 5.7 %collective-permute-done.59 = bf16[2,2,48,384]{3,2,1,0:T(8,128)(2,1)S(1)} collective-permute-done((bf16[2,2,48,384]{3,2,1,0:T(8,128)(2,1)S(1)}, bf16[2,2,48,384]{3,2,1,0:T(8,128)(2,1)S(1)}, u32[]{:S(2)}, u32[]{:S(2)}) %collective-permute-start.59) | collective-permute-done | bytes 147488 | tf_op jit(solution)/shard_map/ppermute | solution.py:68
  273.5 2.3 collective-permute-done.60
  275.9 2.7 collective-permute-start.63
  279.5 2.7 collective-permute-start.51
  287.6 1.5 collective-permute-done.50
  (407 shorter events, 86.3 us)
Async XLA Ops:
  2.7 44.8 %collective-permute-start.9 = (bf16[2,48,768]{2,1,0:T(8,128)(2,1)}, bf16[2,48,768]{2,1,0:T(8,128)(2,1)}, u32[]{:S(2)}, u32[]{:S(2)}) collective-permute-start(bf16[2,48,768]{2,1,0:T(8,128)(2,1)} %get-tuple-element.158), channel_id=1, source_target_pairs={{0,8},{2,10},{4,12},{6,14},{8,0},{10,2},{12,4},{14,6},{1,9},{3,11}... | collective-permute-start | bytes 442376 | tf_op jit(solution)/shard_map/ppermute | solution.py:68
  5.3 46.1 %collective-permute-start.8 = (bf16[2,48,768]{2,1,0:T(8,128)(2,1)}, bf16[2,48,768]{2,1,0:T(8,128)(2,1)}, u32[]{:S(2)}, u32[]{:S(2)}) collective-permute-start(bf16[2,48,768]{2,1,0:T(8,128)(2,1)} %get-tuple-element.158), channel_id=1, source_target_pairs={{0,4},{2,6},{4,8},{6,10},{8,12},{10,14},{12,0},{14,2},{1,5},{3,7},... | collective-permute-start | bytes 442376 | tf_op jit(solution)/shard_map/ppermute | solution.py:68
  9.2 14.7 %collective-permute-start.30 = (bf16[192,80]{0,1:T(8,128)(2,1)S(1)}, bf16[192,80]{0,1:T(8,128)(2,1)S(1)}, u32[]{:S(2)}, u32[]{:S(2)}) collective-permute-start(bf16[192,80]{0,1:T(8,128)(2,1)S(1)} %get-tuple-element.162), channel_id=1, source_target_pairs={{0,8},{2,10},{4,12},{6,14},{8,0},{10,2},{12,4},{14,6},{1,9},{3,11}... | collective-permute-start | bytes 92168 | tf_op jit(solution)/shard_map/ppermute | solution.py:68
  12.1 12.0 %collective-permute-start.29 = (bf16[192,80]{0,1:T(8,128)(2,1)S(1)}, bf16[192,80]{0,1:T(8,128)(2,1)S(1)}, u32[]{:S(2)}, u32[]{:S(2)}) collective-permute-start(bf16[192,80]{0,1:T(8,128)(2,1)S(1)} %get-tuple-element.162), channel_id=1, source_target_pairs={{0,4},{2,6},{4,8},{6,10},{8,12},{10,14},{12,0},{14,2},{1,5},{3,7},... | collective-permute-start | bytes 92168 | tf_op jit(solution)/shard_map/ppermute | solution.py:68
  12.7 11.3 %collective-permute-start.31 = (bf16[192,80]{0,1:T(8,128)(2,1)S(1)}, bf16[192,80]{0,1:T(8,128)(2,1)S(1)}, u32[]{:S(2)}, u32[]{:S(2)}) collective-permute-start(bf16[192,80]{0,1:T(8,128)(2,1)S(1)} %get-tuple-element.162), channel_id=1, source_target_pairs={{0,12},{2,14},{4,0},{6,2},{8,4},{10,6},{12,8},{14,10},{1,13},{3,15... | collective-permute-start | bytes 92168 | tf_op jit(solution)/shard_map/ppermute | solution.py:68
  23.9 11.1 %collective-permute-start.23 = (bf16[2,48,768]{2,1,0:T(8,128)(2,1)}, bf16[2,48,768]{2,1,0:T(8,128)(2,1)S(1)}, u32[]{:S(2)}, u32[]{:S(2)}) collective-permute-start(bf16[2,48,768]{2,1,0:T(8,128)(2,1)} %get-tuple-element.154), channel_id=1, source_target_pairs={{0,8},{2,10},{4,12},{6,14},{8,0},{10,2},{12,4},{14,6},{1,9},{3,11}... | collective-permute-start | bytes 442376 | tf_op jit(solution)/shard_map/ppermute | solution.py:68
  24.0 5.4 %collective-permute-start = (bf16[32,768]{1,0:T(8,128)(2,1)S(1)}, bf16[32,768]{1,0:T(8,128)(2,1)S(1)}, u32[]{:S(2)}, u32[]{:S(2)}) collective-permute-start(bf16[32,768]{1,0:T(8,128)(2,1)S(1)} %get-tuple-element.84), channel_id=1, source_target_pairs={{0,2},{2,4},{4,6},{6,8},{8,10},{10,12},{12,14},{14,0},{1,3},{3,5},... | collective-permute-start | bytes 147464 | tf_op jit(solution)/shard_map/ppermute | solution.py:25
  24.0 9.5 %collective-permute-start.1 = (bf16[32,768]{1,0:T(8,128)(2,1)S(1)}, bf16[32,768]{1,0:T(8,128)(2,1)S(1)}, u32[]{:S(2)}, u32[]{:S(2)}) collective-permute-start(bf16[32,768]{1,0:T(8,128)(2,1)S(1)} %get-tuple-element.85), channel_id=1, source_target_pairs={{2,0},{4,2},{6,4},{8,6},{10,8},{12,10},{14,12},{0,14},{3,1},{5,3},... | collective-permute-start | bytes 147464 | tf_op jit(solution)/shard_map/ppermute | solution.py:27
  29.4 15.5 %collective-permute-start.22 = (bf16[2,48,768]{2,1,0:T(8,128)(2,1)}, bf16[2,48,768]{2,1,0:T(8,128)(2,1)S(1)}, u32[]{:S(2)}, u32[]{:S(2)}) collective-permute-start(bf16[2,48,768]{2,1,0:T(8,128)(2,1)} %get-tuple-element.154), channel_id=1, source_target_pairs={{0,4},{2,6},{4,8},{6,10},{8,12},{10,14},{12,0},{14,2},{1,5},{3,7},... | collective-permute-start | bytes 442376 | tf_op jit(solution)/shard_map/ppermute | solution.py:68
  33.6 11.4 %collective-permute-start.24 = (bf16[2,48,768]{2,1,0:T(8,128)(2,1)}, bf16[2,48,768]{2,1,0:T(8,128)(2,1)S(1)}, u32[]{:S(2)}, u32[]{:S(2)}) collective-permute-start(bf16[2,48,768]{2,1,0:T(8,128)(2,1)} %get-tuple-element.154), channel_id=1, source_target_pairs={{0,12},{2,14},{4,0},{6,2},{8,4},{10,6},{12,8},{14,10},{1,13},{3,15... | collective-permute-start | bytes 442376 | tf_op jit(solution)/shard_map/ppermute | solution.py:68
  35.0 16.4 %collective-permute-start.10 = (bf16[2,48,768]{2,1,0:T(8,128)(2,1)}, bf16[2,48,768]{2,1,0:T(8,128)(2,1)S(1)}, u32[]{:S(2)}, u32[]{:S(2)}) collective-permute-start(bf16[2,48,768]{2,1,0:T(8,128)(2,1)} %get-tuple-element.158), channel_id=1, source_target_pairs={{0,12},{2,14},{4,0},{6,2},{8,4},{10,6},{12,8},{14,10},{1,13},{3,15... | collective-permute-start | bytes 442376 | tf_op jit(solution)/shard_map/ppermute | solution.py:68
  44.9 23.8 %collective-permute-start.17 = (bf16[2,96,384]{2,1,0:T(8,128)(2,1)S(1)}, bf16[2,96,384]{2,1,0:T(8,128)(2,1)S(1)}, u32[]{:S(2)}, u32[]{:S(2)}) collective-permute-start(bf16[2,96,384]{2,1,0:T(8,128)(2,1)S(1)} %copy-done.32), channel_id=1, source_target_pairs={{0,8},{2,10},{4,12},{6,14},{8,0},{10,2},{12,4},{14,6},{1,9},{3,11}... | collective-permute-start | bytes 442376 | tf_op jit(solution)/shard_map/ppermute | solution.py:68
  44.9 25.1 %collective-permute-start.16 = (bf16[2,96,384]{2,1,0:T(8,128)(2,1)S(1)}, bf16[2,96,384]{2,1,0:T(8,128)(2,1)S(1)}, u32[]{:S(2)}, u32[]{:S(2)}) collective-permute-start(bf16[2,96,384]{2,1,0:T(8,128)(2,1)S(1)} %copy-done.32), channel_id=1, source_target_pairs={{0,4},{2,6},{4,8},{6,10},{8,12},{10,14},{12,0},{14,2},{1,5},{3,7},... | collective-permute-start | bytes 442376 | tf_op jit(solution)/shard_map/ppermute | solution.py:68
  47.5 15.5 %collective-permute-start.3 = (bf16[2,96,384]{2,1,0:T(8,128)(2,1)S(1)}, bf16[2,96,384]{2,1,0:T(8,128)(2,1)S(1)}, u32[]{:S(2)}, u32[]{:S(2)}) collective-permute-start(bf16[2,96,384]{2,1,0:T(8,128)(2,1)S(1)} %copy-done.33), channel_id=1, source_target_pairs={{0,8},{2,10},{4,12},{6,14},{8,0},{10,2},{12,4},{14,6},{1,9},{3,11}... | collective-permute-start | bytes 442376 | tf_op jit(solution)/shard_map/ppermute | solution.py:68
  51.4 14.2 %collective-permute-start.2 = (bf16[2,96,384]{2,1,0:T(8,128)(2,1)S(1)}, bf16[2,96,384]{2,1,0:T(8,128)(2,1)S(1)}, u32[]{:S(2)}, u32[]{:S(2)}) collective-permute-start(bf16[2,96,384]{2,1,0:T(8,128)(2,1)S(1)} %copy-done.33), channel_id=1, source_target_pairs={{0,4},{2,6},{4,8},{6,10},{8,12},{10,14},{12,0},{14,2},{1,5},{3,7},... | collective-permute-start | bytes 442376 | tf_op jit(solution)/shard_map/ppermute | solution.py:68
  51.4 15.7 %collective-permute-start.4 = (bf16[2,96,384]{2,1,0:T(8,128)(2,1)S(1)}, bf16[2,96,384]{2,1,0:T(8,128)(2,1)S(1)}, u32[]{:S(2)}, u32[]{:S(2)}) collective-permute-start(bf16[2,96,384]{2,1,0:T(8,128)(2,1)S(1)} %copy-done.33), channel_id=1, source_target_pairs={{0,12},{2,14},{4,0},{6,2},{8,4},{10,6},{12,8},{14,10},{1,13},{3,15... | collective-permute-start | bytes 442376 | tf_op jit(solution)/shard_map/ppermute | solution.py:68
  63.1 7.5 %collective-permute-start.18 = (bf16[2,96,384]{2,1,0:T(8,128)(2,1)S(1)}, bf16[2,96,384]{2,1,0:T(8,128)(2,1)S(1)}, u32[]{:S(2)}, u32[]{:S(2)}) collective-permute-start(bf16[2,96,384]{2,1,0:T(8,128)(2,1)S(1)} %copy-done.32), channel_id=1, source_target_pairs={{0,12},{2,14},{4,0},{6,2},{8,4},{10,6},{12,8},{14,10},{1,13},{3,15... | collective-permute-start | bytes 442376 | tf_op jit(solution)/shard_map/ppermute | solution.py:68
  65.6 9.9 %collective-permute-start.25 = (bf16[4,48,768]{2,1,0:T(8,128)(2,1)S(1)}, bf16[4,48,768]{2,1,0:T(8,128)(2,1)S(1)}, u32[]{:S(2)}, u32[]{:S(2)}) collective-permute-start(bf16[4,48,768]{2,1,0:T(8,128)(2,1)S(1)} %get-tuple-element.104), channel_id=1, source_target_pairs={{0,16},{16,0},{1,17},{17,1},{2,18},{18,2},{3,19},{19,3},{4,20},{20... | collective-permute-start | bytes 884744 | tf_op jit(solution)/shard_map/ppermute | solution.py:57
  67.1 9.9 %collective-permute-start.26 = (bf16[4,48,768]{2,1,0:T(8,128)(2,1)S(1)}, bf16[4,48,768]{2,1,0:T(8,128)(2,1)S(1)}, u32[]{:S(2)}, u32[]{:S(2)}) collective-permute-start(bf16[4,48,768]{2,1,0:T(8,128)(2,1)S(1)} %get-tuple-element.105), channel_id=1, source_target_pairs={{0,1},{1,0},{2,3},{3,2},{4,5},{5,4},{6,7},{7,6},{8,9},{9,8},{10,11... | collective-permute-start | bytes 884744 | tf_op jit(solution)/shard_map/ppermute | solution.py:57
  68.8 26.4 %collective-permute-start.11 = (bf16[4,48,768]{2,1,0:T(8,128)(2,1)S(1)}, bf16[4,48,768]{2,1,0:T(8,128)(2,1)S(1)}, u32[]{:S(2)}, u32[]{:S(2)}) collective-permute-start(bf16[4,48,768]{2,1,0:T(8,128)(2,1)S(1)} %get-tuple-element.118), channel_id=1, source_target_pairs={{0,16},{16,0},{1,17},{17,1},{2,18},{18,2},{3,19},{19,3},{4,20},{20... | collective-permute-start | bytes 884744 | tf_op jit(solution)/shard_map/ppermute | solution.py:57
  70.0 25.2 %collective-permute-start.12 = (bf16[4,48,768]{2,1,0:T(8,128)(2,1)S(1)}, bf16[4,48,768]{2,1,0:T(8,128)(2,1)S(1)}, u32[]{:S(2)}, u32[]{:S(2)}) collective-permute-start(bf16[4,48,768]{2,1,0:T(8,128)(2,1)S(1)} %get-tuple-element.119), channel_id=1, source_target_pairs={{0,1},{1,0},{2,3},{3,2},{4,5},{5,4},{6,7},{7,6},{8,9},{9,8},{10,11... | collective-permute-start | bytes 884744 | tf_op jit(solution)/shard_map/ppermute | solution.py:57
  70.5 17.6 %collective-permute-start.5 = (bf16[4,96,384]{2,1,0:T(8,128)(2,1)S(1)}, bf16[4,96,384]{2,1,0:T(8,128)(2,1)S(1)}, u32[]{:S(2)}, u32[]{:S(2)}) collective-permute-start(bf16[4,96,384]{2,1,0:T(8,128)(2,1)S(1)} %get-tuple-element.122), channel_id=1, source_target_pairs={{0,16},{16,0},{1,17},{17,1},{2,18},{18,2},{3,19},{19,3},{4,20},{20... | collective-permute-start | bytes 884744 | tf_op jit(solution)/shard_map/ppermute | solution.py:57
  75.5 14.2 %collective-permute-start.6 = (bf16[4,96,384]{2,1,0:T(8,128)(2,1)S(1)}, bf16[4,96,384]{2,1,0:T(8,128)(2,1)S(1)}, u32[]{:S(2)}, u32[]{:S(2)}) collective-permute-start(bf16[4,96,384]{2,1,0:T(8,128)(2,1)S(1)} %get-tuple-element.123), channel_id=1, source_target_pairs={{0,1},{1,0},{2,3},{3,2},{4,5},{5,4},{6,7},{7,6},{8,9},{9,8},{10,11... | collective-permute-start | bytes 884744 | tf_op jit(solution)/shard_map/ppermute | solution.py:57
  77.0 16.2 %collective-permute-start.19 = (bf16[4,96,384]{2,1,0:T(8,128)(2,1)S(1)}, bf16[4,96,384]{2,1,0:T(8,128)(2,1)S(1)}, u32[]{:S(2)}, u32[]{:S(2)}) collective-permute-start(bf16[4,96,384]{2,1,0:T(8,128)(2,1)S(1)} %get-tuple-element.112), channel_id=1, source_target_pairs={{0,16},{16,0},{1,17},{17,1},{2,18},{18,2},{3,19},{19,3},{4,20},{20... | collective-permute-start | bytes 884744 | tf_op jit(solution)/shard_map/ppermute | solution.py:57
  88.1 6.7 %collective-permute-start.20 = (bf16[4,96,384]{2,1,0:T(8,128)(2,1)S(1)}, bf16[4,96,384]{2,1,0:T(8,128)(2,1)S(1)}, u32[]{:S(2)}, u32[]{:S(2)}) collective-permute-start(bf16[4,96,384]{2,1,0:T(8,128)(2,1)S(1)} %get-tuple-element.113), channel_id=1, source_target_pairs={{0,1},{1,0},{2,3},{3,2},{4,5},{5,4},{6,7},{7,6},{8,9},{9,8},{10,11... | collective-permute-start | bytes 884744 | tf_op jit(solution)/shard_map/ppermute | solution.py:57
  89.7 6.3 %collective-permute-start.27 = (bf16[4,192,768]{2,1,0:T(8,128)(2,1)S(1)}, bf16[4,192,768]{2,1,0:T(8,128)(2,1)S(1)}, u32[]{:S(2)}, u32[]{:S(2)}) collective-permute-start(bf16[4,192,768]{2,1,0:T(8,128)(2,1)S(1)} %pad_maximum_fusion.3), channel_id=1, source_target_pairs={{0,2},{2,0},{4,6},{6,4},{8,10},{10,8},{12,14},{14,12},{1,3},{3,1},... | collective-permute-start | bytes 3538952 | tf_op jit(solution)/shard_map/ppermute | solution.py:61
  95.4 7.0 %collective-permute-start.13 = (bf16[4,192,768]{2,1,0:T(8,128)(2,1)S(1)}, bf16[4,192,768]{2,1,0:T(8,128)(2,1)S(1)}, u32[]{:S(2)}, u32[]{:S(2)}) collective-permute-start(bf16[4,192,768]{2,1,0:T(8,128)(2,1)S(1)} %pad_maximum_fusion.1), channel_id=1, source_target_pairs={{0,2},{2,0},{4,6},{6,4},{8,10},{10,8},{12,14},{14,12},{1,3},{3,1},... | collective-permute-start | bytes 3538952 | tf_op jit(solution)/shard_map/ppermute | solution.py:61
  104.8 3.8 %collective-permute-start.14 = (bf16[32,768]{1,0:T(8,128)(2,1)S(1)}, bf16[32,768]{1,0:T(8,128)(2,1)S(1)}, u32[]{:S(2)}, u32[]{:S(2)}) collective-permute-start(bf16[32,768]{1,0:T(8,128)(2,1)S(1)} %get-tuple-element.82), channel_id=1, source_target_pairs={{0,2},{2,4},{4,6},{6,8},{8,10},{10,12},{12,14},{14,0},{1,3},{3,5},... | collective-permute-start | bytes 147464 | tf_op jit(solution)/shard_map/ppermute | solution.py:25
  105.0 3.9 %collective-permute-start.15 = (bf16[32,768]{1,0:T(8,128)(2,1)S(1)}, bf16[32,768]{1,0:T(8,128)(2,1)S(1)}, u32[]{:S(2)}, u32[]{:S(2)}) collective-permute-start(bf16[32,768]{1,0:T(8,128)(2,1)S(1)} %get-tuple-element.83), channel_id=1, source_target_pairs={{2,0},{4,2},{6,4},{8,6},{10,8},{12,10},{14,12},{0,14},{3,1},{5,3},... | collective-permute-start | bytes 147464 | tf_op jit(solution)/shard_map/ppermute | solution.py:27
  124.3 5.8 %collective-permute-start.34 = (f32[14]{0:T(128)S(1)}, f32[14]{0:T(128)S(1)}, u32[]{:S(2)}, u32[]{:S(2)}) collective-permute-start(f32[14]{0:T(128)S(1)} %add.515), channel_id=1, source_target_pairs={{0,8},{2,10},{4,12},{6,14},{8,0},{10,2},{12,4},{14,6},{1,9},{3,11}... | collective-permute-start | bytes 176 | tf_op jit(solution)/shard_map/ppermute | solution.py:77
  133.2 8.8 %all-to-all-start = ((f32[1,80,512]{2,0,1:T(1,128)}), f32[1,80,512]{2,0,1:T(1,128)S(1)}, u32[]{:S(2)}, u32[]{:S(2)}) async-start(f32[1,80,512]{2,0,1:T(1,128)} %copy.71), calls=%async_computation | async-start | bytes 327680 | tf_op jit(solution)/shard_map/all_to_all | solution.py:299
  156.7 4.5 %collective-permute-start.37 = (f32[4,20]{1,0:T(4,128)S(1)}, f32[4,20]{1,0:T(4,128)S(1)}, u32[]{:S(2)}, u32[]{:S(2)}) collective-permute-start(f32[4,20]{1,0:T(4,128)S(1)} %add.526), channel_id=1, source_target_pairs={{0,8},{2,10},{4,12},{6,14},{8,0},{10,2},{12,4},{14,6},{1,9},{3,11}... | collective-permute-start | bytes 968 | tf_op jit(solution)/shard_map/ppermute | solution.py:77
  162.6 8.4 %all-to-all-start.1 = ((bf16[4,20,512]{2,1,0:T(8,128)(2,1)}), bf16[4,20,512]{2,1,0:T(8,128)(2,1)S(1)}, u32[]{:S(2)}, u32[]{:S(2)}) async-start(bf16[4,20,512]{2,1,0:T(8,128)(2,1)} %multiply_subtract_fusion), calls=%async_computation.1 | async-start | bytes 196608 | tf_op jit(solution)/shard_map/all_to_all | solution.py:313
  187.3 10.8 %collective-permute-start.64 = (f32[4,96,80]{1,2,0:T(8,128)S(1)}, f32[4,96,80]{1,2,0:T(8,128)S(1)}, u32[]{:S(2)}, u32[]{:S(2)}) collective-permute-start(f32[4,96,80]{1,2,0:T(8,128)S(1)} %bitcast.394), channel_id=1, source_target_pairs={{0,2},{2,0},{4,6},{6,4},{8,10},{10,8},{12,14},{14,12},{1,3},{3,1},... | collective-permute-start | bytes 368648 | tf_op jit(solution)/shard_map/ppermute | solution.py:61
  190.9 26.2 %collective-permute-start.53 = (bf16[384,1536]{1,0:T(8,128)(2,1)S(1)}, bf16[384,1536]{1,0:T(8,128)(2,1)S(1)}, u32[]{:S(2)}, u32[]{:S(2)}) collective-permute-start(bf16[384,1536]{1,0:T(8,128)(2,1)S(1)} %convolution_convert_fusion), channel_id=1, source_target_pairs={{0,2},{2,0},{4,6},{6,4},{8,10},{10,8},{12,14},{14,12},{1,3},{3,1},... | collective-permute-start | bytes 3538952 | tf_op jit(solution)/shard_map/ppermute | solution.py:61
  191.0 25.3 %collective-permute-start.52 = (bf16[768,768]{1,0:T(8,128)(2,1)S(1)}, bf16[768,768]{1,0:T(8,128)(2,1)S(1)}, u32[]{:S(2)}, u32[]{:S(2)}) collective-permute-start(bf16[768,768]{1,0:T(8,128)(2,1)S(1)} %convolution_convert_fusion.2), channel_id=1, source_target_pairs={{0,2},{2,0},{4,6},{6,4},{8,10},{10,8},{12,14},{14,12},{1,3},{3,1},... | collective-permute-start | bytes 3538952 | tf_op jit(solution)/shard_map/ppermute | solution.py:61
  191.5 5.9 %collective-permute-start.39 = (f32[32,768]{1,0:T(8,128)S(1)}, f32[32,768]{1,0:T(8,128)S(1)}, u32[]{:S(2)}, u32[]{:S(2)}) collective-permute-start(f32[32,768]{1,0:T(8,128)S(1)} %copy-done.34), channel_id=1, source_target_pairs={{14,0},{0,2},{2,4},{4,6},{6,8},{8,10},{10,12},{12,14},{15,1},{1,3}... | collective-permute-start | bytes 294920 | tf_op jit(solution)/shard_map/ppermute | solution.py:37
  198.2 9.3 %collective-permute-start.65 = (f32[96,80]{0,1:T(8,128)S(1)}, f32[96,80]{0,1:T(8,128)S(1)}, u32[]{:S(2)}, u32[]{:S(2)}) collective-permute-start(f32[96,80]{0,1:T(8,128)S(1)} %get-tuple-element.130), channel_id=1, source_target_pairs={{0,4},{2,6},{4,8},{6,10},{8,12},{10,14},{12,0},{14,2},{1,5},{3,7},... | collective-permute-start | bytes 92168 | tf_op jit(solution)/shard_map/ppermute | solution.py:68
  198.8 8.7 %collective-permute-start.67 = (f32[96,80]{0,1:T(8,128)S(1)}, f32[96,80]{0,1:T(8,128)S(1)}, u32[]{:S(2)}, u32[]{:S(2)}) collective-permute-start(f32[96,80]{0,1:T(8,128)S(1)} %get-tuple-element.131), channel_id=1, source_target_pairs={{0,12},{2,14},{4,0},{6,2},{8,4},{10,6},{12,8},{14,10},{1,13},{3,15... | collective-permute-start | bytes 92168 | tf_op jit(solution)/shard_map/ppermute | solution.py:68
  202.1 5.4 %collective-permute-start.66 = (f32[96,80]{0,1:T(8,128)S(1)}, f32[96,80]{0,1:T(8,128)S(1)}, u32[]{:S(2)}, u32[]{:S(2)}) collective-permute-start(f32[96,80]{0,1:T(8,128)S(1)} %get-tuple-element.132), channel_id=1, source_target_pairs={{0,8},{2,10},{4,12},{6,14},{8,0},{10,2},{12,4},{14,6},{1,9},{3,11}... | collective-permute-start | bytes 92168 | tf_op jit(solution)/shard_map/ppermute | solution.py:68
  207.5 4.1 %collective-permute-start.68 = (f32[96,80]{0,1:T(8,128)S(1)}, f32[96,80]{0,1:T(8,128)S(1)}, u32[]{:S(2)}, u32[]{:S(2)}) collective-permute-start(f32[96,80]{0,1:T(8,128)S(1)} %fusion.84), channel_id=1, source_target_pairs={{0,16},{16,0},{1,17},{17,1},{2,18},{18,2},{3,19},{19,3},{4,20},{20... | collective-permute-start | bytes 92168 | tf_op jit(solution)/shard_map/ppermute | solution.py:57
  211.6 4.0 %collective-permute-start.69 = (f32[96,80]{0,1:T(8,128)S(1)}, f32[96,80]{0,1:T(8,128)S(1)}, u32[]{:S(2)}, u32[]{:S(2)}) collective-permute-start(f32[96,80]{0,1:T(8,128)S(1)} %add.569), channel_id=1, source_target_pairs={{0,1},{1,0},{2,3},{3,2},{4,5},{5,4},{6,7},{7,6},{8,9},{9,8},{10,11... | collective-permute-start | bytes 92168 | tf_op jit(solution)/shard_map/ppermute | solution.py:57
  213.2 6.7 %collective-permute-start.41 = (bf16[384,1536]{1,0:T(8,128)(2,1)S(1)}, bf16[384,1536]{1,0:T(8,128)(2,1)S(1)}, u32[]{:S(2)}, u32[]{:S(2)}) collective-permute-start(bf16[384,1536]{1,0:T(8,128)(2,1)S(1)} %convolution_convert_fusion.1), channel_id=1, source_target_pairs={{0,2},{2,0},{4,6},{6,4},{8,10},{10,8},{12,14},{14,12},{1,3},{3,1},... | collective-permute-start | bytes 3538952 | tf_op jit(solution)/shard_map/ppermute | solution.py:61
  213.3 7.4 %collective-permute-start.40 = (bf16[768,768]{1,0:T(8,128)(2,1)S(1)}, bf16[768,768]{1,0:T(8,128)(2,1)S(1)}, u32[]{:S(2)}, u32[]{:S(2)}) collective-permute-start(bf16[768,768]{1,0:T(8,128)(2,1)S(1)} %convolution_convert_fusion.3), channel_id=1, source_target_pairs={{0,2},{2,0},{4,6},{6,4},{8,10},{10,8},{12,14},{14,12},{1,3},{3,1},... | collective-permute-start | bytes 3538952 | tf_op jit(solution)/shard_map/ppermute | solution.py:61
  218.3 16.3 %collective-permute-start.54 = (bf16[2,4,48,768]{3,2,1,0:T(8,128)(2,1)S(1)}, bf16[2,4,48,768]{3,2,1,0:T(8,128)(2,1)S(1)}, u32[]{:S(2)}, u32[]{:S(2)}) collective-permute-start(bf16[2,4,48,768]{3,2,1,0:T(8,128)(2,1)S(1)} %fusion.22), channel_id=1, source_target_pairs={{0,16},{16,0},{1,17},{17,1},{2,18},{18,2},{3,19},{19,3},{4,20},{20... | collective-permute-start | bytes 1769480 | tf_op jit(solution)/shard_map/ppermute | solution.py:57
  219.2 16.5 %collective-permute-start.56 = (bf16[2,4,48,768]{3,2,0,1:T(8,128)(2,1)S(1)}, bf16[2,4,48,768]{3,2,0,1:T(8,128)(2,1)S(1)}, u32[]{:S(2)}, u32[]{:S(2)}) collective-permute-start(bf16[2,4,48,768]{3,2,0,1:T(8,128)(2,1)S(1)} %fusion.18), channel_id=1, source_target_pairs={{0,1},{1,0},{2,3},{3,2},{4,5},{5,4},{6,7},{7,6},{8,9},{9,8},{10,11... | collective-permute-start | bytes 1769480 | tf_op jit(solution)/shard_map/ppermute | solution.py:57
  222.2 25.0 %collective-permute-start.42 = (bf16[2,4,48,768]{3,2,1,0:T(8,128)(2,1)S(1)}, bf16[2,4,48,768]{3,2,1,0:T(8,128)(2,1)S(1)}, u32[]{:S(2)}, u32[]{:S(2)}) collective-permute-start(bf16[2,4,48,768]{3,2,1,0:T(8,128)(2,1)S(1)} %fusion.30), channel_id=1, source_target_pairs={{0,16},{16,0},{1,17},{17,1},{2,18},{18,2},{3,19},{19,3},{4,20},{20... | collective-permute-start | bytes 1769480 | tf_op jit(solution)/shard_map/ppermute | solution.py:57
  223.8 24.5 %collective-permute-start.44 = (bf16[2,4,48,768]{3,2,0,1:T(8,128)(2,1)S(1)}, bf16[2,4,48,768]{3,2,0,1:T(8,128)(2,1)S(1)}, u32[]{:S(2)}, u32[]{:S(2)}) collective-permute-start(bf16[2,4,48,768]{3,2,0,1:T(8,128)(2,1)S(1)} %fusion.26), channel_id=1, source_target_pairs={{0,1},{1,0},{2,3},{3,2},{4,5},{5,4},{6,7},{7,6},{8,9},{9,8},{10,11... | collective-permute-start | bytes 1769480 | tf_op jit(solution)/shard_map/ppermute | solution.py:57
  234.8 19.6 %collective-permute-start.55 = (bf16[2,4,48,384]{3,2,1,0:T(8,128)(2,1)S(1)}, bf16[2,4,48,384]{3,2,1,0:T(8,128)(2,1)S(1)}, u32[]{:S(2)}, u32[]{:S(2)}) collective-permute-start(bf16[2,4,48,384]{3,2,1,0:T(8,128)(2,1)S(1)} %dynamic-slice_convert_fusion.1), channel_id=1, source_target_pairs={{0,1},{1,0},{2,3},{3,2},{4,5},{5,4},{6,7},{7,6},{8,9},{9,8},{10,11... | collective-permute-start | bytes 884744 | tf_op jit(solution)/shard_map/ppermute | solution.py:57
  235.9 18.6 %collective-permute-start.57 = (bf16[2,4,48,384]{3,2,0,1:T(8,128)(2,1)S(1)}, bf16[2,4,48,384]{3,2,0,1:T(8,128)(2,1)S(1)}, u32[]{:S(2)}, u32[]{:S(2)}) collective-permute-start(bf16[2,4,48,384]{3,2,0,1:T(8,128)(2,1)S(1)} %dynamic-slice_convert_fusion), channel_id=1, source_target_pairs={{0,16},{16,0},{1,17},{17,1},{2,18},{18,2},{3,19},{19,3},{4,20},{20... | collective-permute-start | bytes 884744 | tf_op jit(solution)/shard_map/ppermute | solution.py:57
  247.5 12.8 %collective-permute-start.43 = (bf16[2,4,48,384]{3,2,1,0:T(8,128)(2,1)S(1)}, bf16[2,4,48,384]{3,2,1,0:T(8,128)(2,1)S(1)}, u32[]{:S(2)}, u32[]{:S(2)}) collective-permute-start(bf16[2,4,48,384]{3,2,1,0:T(8,128)(2,1)S(1)} %dynamic-slice_convert_fusion.3), channel_id=1, source_target_pairs={{0,1},{1,0},{2,3},{3,2},{4,5},{5,4},{6,7},{7,6},{8,9},{9,8},{10,11... | collective-permute-start | bytes 884744 | tf_op jit(solution)/shard_map/ppermute | solution.py:57
  248.5 11.8 %collective-permute-start.45 = (bf16[2,4,48,384]{3,2,0,1:T(8,128)(2,1)S(1)}, bf16[2,4,48,384]{3,2,0,1:T(8,128)(2,1)S(1)}, u32[]{:S(2)}, u32[]{:S(2)}) collective-permute-start(bf16[2,4,48,384]{3,2,0,1:T(8,128)(2,1)S(1)} %dynamic-slice_convert_fusion.2), channel_id=1, source_target_pairs={{0,16},{16,0},{1,17},{17,1},{2,18},{18,2},{3,19},{19,3},{4,20},{20... | collective-permute-start | bytes 884744 | tf_op jit(solution)/shard_map/ppermute | solution.py:57
  254.6 13.2 %collective-permute-start.58 = (bf16[2,2,48,384]{3,2,1,0:T(8,128)(2,1)S(1)}, bf16[2,2,48,384]{3,2,1,0:T(8,128)(2,1)S(1)}, u32[]{:S(2)}, u32[]{:S(2)}) collective-permute-start(bf16[2,2,48,384]{3,2,1,0:T(8,128)(2,1)S(1)} %get-tuple-element.59), channel_id=1, source_target_pairs={{0,4},{2,6},{4,8},{6,10},{8,12},{10,14},{12,0},{14,2},{1,5},{3,7},... | collective-permute-start | bytes 442376 | tf_op jit(solution)/shard_map/ppermute | solution.py:68
  257.5 16.0 %collective-permute-start.59 = (bf16[2,2,48,384]{3,2,1,0:T(8,128)(2,1)S(1)}, bf16[2,2,48,384]{3,2,1,0:T(8,128)(2,1)S(1)}, u32[]{:S(2)}, u32[]{:S(2)}) collective-permute-start(bf16[2,2,48,384]{3,2,1,0:T(8,128)(2,1)S(1)} %get-tuple-element.60), channel_id=1, source_target_pairs={{0,8},{2,10},{4,12},{6,14},{8,0},{10,2},{12,4},{14,6},{1,9},{3,11}... | collective-permute-start | bytes 442376 | tf_op jit(solution)/shard_map/ppermute | solution.py:68
  260.2 15.6 %collective-permute-start.60 = (bf16[2,2,48,384]{3,2,1,0:T(8,128)(2,1)S(1)}, bf16[2,2,48,384]{3,2,1,0:T(8,128)(2,1)S(1)}, u32[]{:S(2)}, u32[]{:S(2)}) collective-permute-start(bf16[2,2,48,384]{3,2,1,0:T(8,128)(2,1)S(1)} %get-tuple-element.61), channel_id=1, source_target_pairs={{0,12},{2,14},{4,0},{6,2},{8,4},{10,6},{12,8},{14,10},{1,13},{3,15... | collective-permute-start | bytes 442376 | tf_op jit(solution)/shard_map/ppermute | solution.py:68
  260.5 18.6 %collective-permute-start.46 = (bf16[2,2,48,384]{3,2,1,0:T(8,128)(2,1)S(1)}, bf16[2,2,48,384]{3,2,1,0:T(8,128)(2,1)S(1)}, u32[]{:S(2)}, u32[]{:S(2)}) collective-permute-start(bf16[2,2,48,384]{3,2,1,0:T(8,128)(2,1)S(1)} %get-tuple-element.56), channel_id=1, source_target_pairs={{0,4},{2,6},{4,8},{6,10},{8,12},{10,14},{12,0},{14,2},{1,5},{3,7},... | collective-permute-start | bytes 442376 | tf_op jit(solution)/shard_map/ppermute | solution.py:68
  262.5 16.9 %collective-permute-start.47 = (bf16[2,2,48,384]{3,2,1,0:T(8,128)(2,1)S(1)}, bf16[2,2,48,384]{3,2,1,0:T(8,128)(2,1)S(1)}, u32[]{:S(2)}, u32[]{:S(2)}) collective-permute-start(bf16[2,2,48,384]{3,2,1,0:T(8,128)(2,1)S(1)} %get-tuple-element.57), channel_id=1, source_target_pairs={{0,8},{2,10},{4,12},{6,14},{8,0},{10,2},{12,4},{14,6},{1,9},{3,11}... | collective-permute-start | bytes 442376 | tf_op jit(solution)/shard_map/ppermute | solution.py:68
  267.8 11.7 %collective-permute-start.48 = (bf16[2,2,48,384]{3,2,1,0:T(8,128)(2,1)S(1)}, bf16[2,2,48,384]{3,2,1,0:T(8,128)(2,1)S(1)}, u32[]{:S(2)}, u32[]{:S(2)}) collective-permute-start(bf16[2,2,48,384]{3,2,1,0:T(8,128)(2,1)S(1)} %get-tuple-element.58), channel_id=1, source_target_pairs={{0,12},{2,14},{4,0},{6,2},{8,4},{10,6},{12,8},{14,10},{1,13},{3,15... | collective-permute-start | bytes 442376 | tf_op jit(solution)/shard_map/ppermute | solution.py:68
  275.9 7.3 %collective-permute-start.63 = (bf16[2,2,48,384]{3,2,1,0:T(8,128)(2,1)S(1)}, bf16[2,2,48,384]{3,2,1,0:T(8,128)(2,1)S(1)}, u32[]{:S(2)}, u32[]{:S(2)}) collective-permute-start(bf16[2,2,48,384]{3,2,1,0:T(8,128)(2,1)S(1)} %fusion.57), channel_id=1, source_target_pairs={{0,17},{1,16},{16,1},{17,0},{2,19},{3,18},{18,3},{19,2},{4,21},{5,... | collective-permute-start | bytes 442376 | tf_op jit(solution)/shard_map/ppermute | solution.py:179
  278.6 7.3 %collective-permute-start.62 = (bf16[2,2,48,384]{3,2,1,0:T(8,128)(2,1)S(1)}, bf16[2,2,48,384]{3,2,1,0:T(8,128)(2,1)S(1)}, u32[]{:S(2)}, u32[]{:S(2)}) collective-permute-start(bf16[2,2,48,384]{3,2,1,0:T(8,128)(2,1)S(1)} %fusion.57), channel_id=1, source_target_pairs={{0,1},{1,0},{16,17},{17,16},{2,3},{3,2},{18,19},{19,18},{4,5},{5,4... | collective-permute-start | bytes 442376 | tf_op jit(solution)/shard_map/ppermute | solution.py:179
  279.1 8.0 %collective-permute-start.61 = (bf16[2,2,48,384]{3,2,1,0:T(8,128)(2,1)S(1)}, bf16[2,2,48,384]{3,2,1,0:T(8,128)(2,1)S(1)}, u32[]{:S(2)}, u32[]{:S(2)}) collective-permute-start(bf16[2,2,48,384]{3,2,1,0:T(8,128)(2,1)S(1)} %fusion.57), channel_id=1, source_target_pairs={{0,16},{1,17},{16,0},{17,1},{2,18},{3,19},{18,2},{19,3},{4,20},{5,... | collective-permute-start | bytes 442376 | tf_op jit(solution)/shard_map/ppermute | solution.py:179
  279.5 8.1 %collective-permute-start.51 = (bf16[2,2,48,384]{3,2,1,0:T(8,128)(2,1)S(1)}, bf16[2,2,48,384]{3,2,1,0:T(8,128)(2,1)S(1)}, u32[]{:S(2)}, u32[]{:S(2)}) collective-permute-start(bf16[2,2,48,384]{3,2,1,0:T(8,128)(2,1)S(1)} %fusion.69), channel_id=1, source_target_pairs={{0,17},{1,16},{16,1},{17,0},{2,19},{3,18},{18,3},{19,2},{4,21},{5,... | collective-permute-start | bytes 442376 | tf_op jit(solution)/shard_map/ppermute | solution.py:179
  282.3 6.8 %collective-permute-start.50 = (bf16[2,2,48,384]{3,2,1,0:T(8,128)(2,1)S(1)}, bf16[2,2,48,384]{3,2,1,0:T(8,128)(2,1)S(1)}, u32[]{:S(2)}, u32[]{:S(2)}) collective-permute-start(bf16[2,2,48,384]{3,2,1,0:T(8,128)(2,1)S(1)} %fusion.69), channel_id=1, source_target_pairs={{0,1},{1,0},{16,17},{17,16},{2,3},{3,2},{18,19},{19,18},{4,5},{5,4... | collective-permute-start | bytes 442376 | tf_op jit(solution)/shard_map/ppermute | solution.py:179
  283.2 7.1 %collective-permute-start.49 = (bf16[2,2,48,384]{3,2,1,0:T(8,128)(2,1)S(1)}, bf16[2,2,48,384]{3,2,1,0:T(8,128)(2,1)S(1)}, u32[]{:S(2)}, u32[]{:S(2)}) collective-permute-start(bf16[2,2,48,384]{3,2,1,0:T(8,128)(2,1)S(1)} %fusion.69), channel_id=1, source_target_pairs={{0,16},{1,17},{16,0},{17,1},{2,18},{3,19},{18,2},{19,3},{4,20},{5,... | collective-permute-start | bytes 442376 | tf_op jit(solution)/shard_map/ppermute | solution.py:179
  (69 other events, 1211.5 us)
